TPU v7x, 32 devices: a whole 2x2x4 slice. The times are simulated.
32 devices in a mesh: leaf: 32 (over z, y, x, core).
Axes of the slice: x: 2, y: 2, z: 4, core: 2. Of those that a mesh axis runs over, the one named last changes fastest.
Arguments:
- coords: float32 [6, 262144], P(None, 'leaf'), may hold values from 0 to 4
- right_sides: float32 [8, 262144], P(None, 'leaf'), may hold values from -6 to 6
- projection: float32 [262144, 256], P('leaf'), may hold values from -0.0625 to 0.0625
- skel_index: int32 [32, 256], P('leaf'), may hold values from 0 to 8191
- selection: int32 [30, 256], replicated, may hold values from 0 to 511
- transfer: float32 [512, 256], replicated, may hold values from -0.25 to 0.25
- near_leaf: int32 [1024, 8], P('leaf'), may hold values from 0 to 1023, as said below
- near_count: int32 [1024], P('leaf'), may hold values from 1 to 8, as said below
Outputs:
- product: float32 [8, 262144], P(None, 'leaf')
Inputs may be any that keep to these rules, and one draw needn't show every extreme that they name: `near_leaf`: slot 0 of leaf g is g itself; every listed leaf is held by the device subtree of g or by one of the two subtrees next to it. `near_count`: all leaves of some device subtrees use all 8 slots; the others use up to 4.
All inputs are finite; a program needn't handle non-finite values.
Results may differ from a plain program's by a relative error of at most 0.0003.
Values sent between devices are 32-bit elements; how exact they have to be, the bound alone decides.
No kernel may reach another device: no remote copies, remote signals or barrier semaphores. Data moves between devices by JAX's collectives and lax.ppermute only.
A program may use at most 192 MiB of HBM per device.

v0:
```python
import functools
import math

import jax
import jax.numpy as jnp
from jax import lax
from jax.experimental import pallas as pl
from jax.experimental.pallas import tpu as pltpu
from jax.sharding import PartitionSpec as P

F32 = jnp.float32
BF16 = jnp.bfloat16
LANES = 128
SHIFT = 2.0
LEAVES_TURN = 4
LEAVES_SELF = 8
ROOT = math.sqrt(math.log2(math.e))
SMEM_SPEC = pl.BlockSpec(memory_space=pltpu.SMEM)
HBM_SPEC = pl.BlockSpec(memory_space=pltpu.HBM)
VMEM_SPEC = pl.BlockSpec(memory_space=pltpu.VMEM)


def swap(value, axis, first):
    count = lax.axis_size(axis)
    pairs = []
    for left in range(first, count - 1, 2):
        pairs += [(left, left + 1), (left + 1, left)]
    return lax.ppermute(value, axis, pairs)


def two_pieces(value):
    high = value.astype(BF16).astype(F32)
    return high, value - high


def three_pieces(value):
    high, rest = two_pieces(value)
    middle, low = two_pieces(rest)
    return high, middle, low


def source_form(extended):
    high, middle, low = three_pieces(extended)
    return jnp.concatenate([high, high, high, middle, middle, low], axis=0).astype(BF16)


def target_form(extended):
    row = lax.broadcasted_iota(jnp.int32, extended.shape, 0)
    below = pltpu.roll(extended, 1, 0)
    swapped = jnp.where(row == 6, 1.0, jnp.where(row == 7, below, extended))
    high, middle, low = three_pieces(swapped)
    return jnp.concatenate([high, middle, low, high, middle, high], axis=0).astype(BF16)


def weight_form(values):
    high, low = two_pieces(values)
    return jnp.concatenate([high, low], axis=0).astype(BF16)


def pick_columns(pieces, index):
    index = jnp.broadcast_to(index, (8, LANES))
    low = index & (LANES - 1)
    high = index >> 7
    result = jnp.take_along_axis(pieces[0], low, axis=1)
    for at in range(1, len(pieces)):
        result = jnp.where(high == at, jnp.take_along_axis(pieces[at], low, axis=1), result)
    return result


def split_block(exponent):
    kernel = jnp.exp2(exponent)
    high = jnp.minimum(kernel.astype(BF16), jnp.ones((), BF16))
    return high, (kernel - high.astype(F32)).astype(BF16)


def kernel_term(source, target, weight, rows):
    highs, lows = [], []
    for first in range(0, source.shape[0], rows):
        high, low = split_block(jnp.dot(source[first:first + rows], target, preferred_element_type=F32))
        highs.append(high)
        lows.append(low)
    high = jnp.concatenate(highs, axis=0) if len(highs) > 1 else highs[0]
    low = jnp.concatenate(lows, axis=0) if len(lows) > 1 else lows[0]
    both = jnp.dot(weight, high, preferred_element_type=F32)
    return both + jnp.dot(weight, low, preferred_element_type=F32)


def fold(pieces):
    return pieces[:8] + pieces[8:]


def extend_kernel(coords_ref, right_ref, index_hbm, out_ref, index_ref, held, sems):
    rows, points = held.shape
    copies = [
        pltpu.make_async_copy(coords_ref, held, sems.at[0]),
        pltpu.make_async_copy(right_ref, out_ref.at[pl.ds(8, 8)], sems.at[1]),
        pltpu.make_async_copy(index_hbm, index_ref, sems.at[2]),
    ]
    for copy in copies:
        copy.start()
    copies[0].wait()
    centred = (held[...] - SHIFT) * ROOT
    out_ref[0:rows, :] = centred
    out_ref[rows:rows + 1, :] = -0.5 * jnp.sum(centred * centred, axis=0, keepdims=True)
    out_ref[rows + 1:rows + 2, :] = jnp.ones((1, points), F32)
    copies[1].wait()
    copies[2].wait()


def extend(coords, right_sides, skel_index):
    rows, points = coords.shape
    return pl.pallas_call(
        extend_kernel,
        out_shape=(pltpu.VMEM((16, points), F32), pltpu.VMEM(skel_index.shape, jnp.int32)),
        in_specs=[HBM_SPEC] * 3,
        out_specs=(VMEM_SPEC, VMEM_SPEC),
        scratch_shapes=[pltpu.VMEM((rows, points), F32), pltpu.SemaphoreType.DMA((3,))],
        compiler_params=pltpu.CompilerParams(vmem_limit_bytes=58 * 2**20),
        name="extend",
    )(coords, right_sides, skel_index)


def first_kernel(leaf, x_ref, proj_ref, index_ref, node_ref, self_ref, held, sources, weights, targets, sems):
    chunks = held.shape[0]
    chunk, rank = held.shape[1:]
    points = x_ref.shape[1]
    copies = [
        pltpu.make_async_copy(proj_ref.at[pl.ds(at * chunk, chunk)], held.at[at], sems.at[at]) for at in range(chunks)
    ]
    for copy in copies:
        copy.start()
    for half in range(rank // LANES):
        lanes = slice(half * LANES, (half + 1) * LANES)
        pieces = [x_ref[0:8, at * LANES:(at + 1) * LANES] for at in range(points // LANES)]
        columns = pick_columns(pieces, index_ref[:, lanes])
        for copy in range(node_ref.shape[0]):
            node_ref[copy, 0:8, lanes] = columns
    wide = 4 * leaf

    def prepare(at, _):
        columns = pl.ds(pl.multiple_of(at * wide, wide), wide)
        sources[:, columns] = source_form(x_ref[0:8, columns])
        weights[:, columns] = weight_form(x_ref[8:16, columns])
        targets[:, columns] = target_form(x_ref[0:8, columns])
        return 0

    def turn(at, _):
        for part in range(LEAVES_SELF):
            columns = pl.ds(pl.multiple_of((at * LEAVES_SELF + part) * leaf, leaf), leaf)
            self_ref[:, columns] = fold(kernel_term(sources[:, columns].T, targets[:, columns], weights[:, columns], 128))
        return 0

    lax.fori_loop(0, points // wide, prepare, 0)
    lax.fori_loop(0, points // (leaf * LEAVES_SELF), turn, 0)
    total = jnp.zeros((8, rank), F32)
    for at in range(chunks):
        x_high, x_low = two_pieces(x_ref[8:16, at * chunk:(at + 1) * chunk])
        left = jnp.concatenate([x_high, x_low], axis=0).astype(BF16)
        copies[at].wait()
        p_high, p_low = two_pieces(held[at])
        both = jnp.dot(left, p_high.astype(BF16), preferred_element_type=F32)
        part = jnp.dot(left, p_low.astype(BF16), preferred_element_type=F32)
        total += both[:8] + both[8:] + part[:8]
    for copy in range(node_ref.shape[0]):
        node_ref[copy, 8:16, :] = total


def first_step(copies, leaf, extended, projection, skel_index):
    points, rank = projection.shape
    chunks = 8
    return pl.pallas_call(
        functools.partial(first_kernel, leaf),
        out_shape=(
            jax.ShapeDtypeStruct((copies, 16, rank), F32),
            jax.ShapeDtypeStruct((8, points), F32),
        ),
        in_specs=[VMEM_SPEC, HBM_SPEC, VMEM_SPEC],
        out_specs=(VMEM_SPEC, VMEM_SPEC),
        scratch_shapes=[
            pltpu.VMEM((chunks, points // chunks, rank), F32),
            pltpu.VMEM((48, points), BF16),
            pltpu.VMEM((16, points), BF16),
            pltpu.VMEM((48, points), BF16),
            pltpu.SemaphoreType.DMA((chunks,)),
        ],
        compiler_params=pltpu.CompilerParams(vmem_limit_bytes=50 * 2**20),
        name="first_step",
    )(extended, projection, skel_index)


def climb(source, first, count, selection, rows, transfer, target, offset):
    rank = transfer[0].shape[1]
    t_high, t_low = transfer
    joined = jnp.concatenate(
        [
            jnp.concatenate([source[first + 2 * m + side, 8:16, :] for m in range(count)], axis=0)
            for side in range(2)
        ],
        axis=1,
    )
    high, low = two_pieces(joined)
    left = jnp.concatenate([high, low], axis=0).astype(BF16)
    both = jnp.dot(left, t_high, preferred_element_type=F32)
    part = jnp.dot(left, t_low, preferred_element_type=F32)
    moved = both[:8 * count] + both[8 * count:] + part[:8 * count]
    for m in range(count):
        target[offset + m, 8:16, :] = moved[m * 8:(m + 1) * 8, :]
        pieces = [
            source[first + 2 * m + side, 0:8, at * LANES:(at + 1) * LANES]
            for side in range(2)
            for at in range(rank // LANES)
        ]
        picked = selection[pl.ds(rows + m, 1), :]
        for half in range(rank // LANES):
            lanes = slice(half * LANES, (half + 1) * LANES)
            target[offset + m, 0:8, lanes] = pick_columns(pieces, picked[:, lanes])


def split_transfer(transfer_ref):
    t_high, t_low = two_pieces(transfer_ref[...])
    return t_high.astype(BF16), t_low.astype(BF16)


def near_kernel(near_ref, count_ref, self_ref, chip_ref, own_ref, other_ref, out_ref, sources, weights, targets):
    leaves, slots = near_ref.shape
    points = own_ref.shape[1]
    leaf = points // leaves
    own_index = lax.axis_index("leaf")
    even = own_index % 2 == 0
    first_leaf = own_index * leaves
    wide = 4 * leaf

    def prepare(at, _):
        columns = pl.ds(pl.multiple_of(at * wide, wide), wide)
        for part, ref in enumerate((chip_ref, own_ref, other_ref)):
            window = pl.ds(pl.multiple_of(part * points + at * wide, wide), wide)
            sources[:, window] = source_form(ref[0:8, columns])
            weights[:, window] = weight_form(ref[8:16, columns])
        targets[:, columns] = target_form(own_ref[0:8, columns])
        return 0

    lax.fori_loop(0, points // wide, prepare, 0)

    def window_place(offset):
        below, above = offset < 0, offset >= leaves
        left = jnp.where(even, 2, 0)
        part = jnp.where(below, left, jnp.where(above, 2 - left, 1))
        local = jnp.where(below, offset + leaves, jnp.where(above, offset - leaves, offset))
        return part * leaves + jnp.clip(local, 0, leaves - 1)

    def one_leaf(at, live_slots):
        columns = pl.ds(pl.multiple_of(at * leaf, leaf), leaf)
        target = targets[:, columns]
        total = jnp.zeros((16, leaf), F32)
        for slot in range(1, live_slots):
            place = window_place(near_ref[at, slot] - first_leaf)
            window = pl.ds(pl.multiple_of(place * leaf, leaf), leaf)
            weight = weights[:, window]
            weight = jnp.where(slot < count_ref[at], weight, jnp.zeros_like(weight))
            total += kernel_term(sources[:, window].T, target, weight, 128)
        out_ref[:, columns] = self_ref[:, columns] + fold(total)

    def turn(at, _):
        most = count_ref[LEAVES_TURN * at]
        for leaf_at in range(1, LEAVES_TURN):
            most = jnp.maximum(most, count_ref[LEAVES_TURN * at + leaf_at])
        heavy = most > slots // 2

        @pl.when(heavy)
        def _():
            for leaf_at in range(LEAVES_TURN):
                one_leaf(LEAVES_TURN * at + leaf_at, slots)

        @pl.when(jnp.logical_not(heavy))
        def _():
            for leaf_at in range(LEAVES_TURN):
                one_leaf(LEAVES_TURN * at + leaf_at, slots // 2)

        return 0

    lax.fori_loop(0, leaves // LEAVES_TURN, turn, 0)


def near_term(near_leaf, near_count, own_part, chip, own, other):
    leaves, slots = near_leaf.shape
    points = own.shape[1]
    entries = leaves * slots * (points // leaves) ** 2
    return pl.pallas_call(
        near_kernel,
        out_shape=jax.ShapeDtypeStruct((8, points), F32),
        in_specs=[SMEM_SPEC] * 2 + [VMEM_SPEC] * 4,
        out_specs=VMEM_SPEC,
        scratch_shapes=[
            pltpu.VMEM((48, 3 * points), BF16),
            pltpu.VMEM((16, 3 * points), BF16),
            pltpu.VMEM((48, points), BF16),
        ],
        cost_estimate=pl.CostEstimate(flops=1000 * entries, bytes_accessed=4 * 64 * points, transcendentals=entries),
        compiler_params=pltpu.CompilerParams(vmem_limit_bytes=32 * 2**20),
        name="near_term",
    )(near_leaf, near_count, own_part, chip, own, other)


def far_kernel(scale, tile, own_ref, near_ref, gathered_ref, selection_ref, transfer_ref, out_ref, nodes, sources, weights):
    devices = gathered_ref.shape[0]
    levels = devices.bit_length() - 1
    own_index = lax.axis_index("leaf")
    transfer = split_transfer(transfer_ref)
    rank = transfer_ref.shape[1]
    held, first = gathered_ref, 0
    for level in range(levels):
        node = held[first + ((own_index >> level) ^ 1)]
        form = source_form(node[0:8])
        sources[level] = jnp.concatenate([form, jnp.zeros((LANES - 48, rank), BF16)], axis=0).T
        weights[level] = weight_form(node[8:16])
        if level < levels - 1:
            rows = devices - (devices >> level)
            climb(held, first, devices >> (level + 1), selection_ref, rows, transfer, nodes, rows)
            held, first = nodes, rows

    def turn(at, _):
        for part in range(LEAVES_TURN):
            columns = pl.ds(pl.multiple_of((at * LEAVES_TURN + part) * tile, tile), tile)
            target = target_form(own_ref[0:8, columns])
            target = jnp.concatenate([target, jnp.zeros((LANES - 48, tile), BF16)], axis=0)
            total = jnp.zeros((16, tile), F32)
            for level in range(levels):
                total += kernel_term(sources[level], target, weights[level], rank)
            out_ref[:, columns] = (fold(total) + near_ref[:, columns]) * scale
        return 0

    lax.fori_loop(0, own_ref.shape[1] // (tile * LEAVES_TURN), turn, 0)


def far_term(scale, tile, own, near, gathered, selection, transfer):
    devices, _, rank = gathered.shape
    levels = devices.bit_length() - 1
    return pl.pallas_call(
        functools.partial(far_kernel, scale, tile),
        out_shape=jax.ShapeDtypeStruct((8, own.shape[1]), F32),
        in_specs=[VMEM_SPEC] * 5,
        out_specs=VMEM_SPEC,
        scratch_shapes=[
            pltpu.VMEM((devices - 2, 16, rank), F32),
            pltpu.VMEM((levels, rank, LANES), BF16),
            pltpu.VMEM((levels, 16, rank), BF16),
        ],
        compiler_params=pltpu.CompilerParams(vmem_limit_bytes=32 * 2**20),
        name="far_term",
    )(own, near, gathered, selection, transfer)


def body(coords, right_sides, projection, skel_index, selection, transfer, near_leaf, near_count):
    devices = lax.axis_size("leaf")
    leaves, slots = near_leaf.shape
    leaf = coords.shape[1] // leaves
    scale = 1.0 / (slots * leaf) ** 0.5
    extended, skel_index = extend(coords, right_sides, skel_index)
    chip = swap(extended, "leaf", 0)
    other = swap(extended, "leaf", 1)
    node, own_part = first_step(devices, leaf, extended, projection, skel_index)
    gathered = lax.all_to_all(node, "leaf", 0, 0, tiled=True)
    near = near_term(near_leaf, near_count, own_part, chip, extended, other)
    return far_term(scale, leaf, extended, near, gathered, selection, transfer)


def solution(mesh):
    return jax.shard_map(
        body,
        mesh=mesh,
        in_specs=(
            P(None, "leaf"),
            P(None, "leaf"),
            P("leaf", None),
            P("leaf", None),
            P(),
            P(),
            P("leaf", None),
            P("leaf"),
        ),
        out_specs=P(None, "leaf"),
        check_vma=False,
    )
```

profile of v0, /device:TPU:0, one launch (start us, length us, event | category | flops | bytes accessed | tf_op | source)
XLA Modules:
  0.0 52.3 jit_solution(15512743031592361357)
XLA Ops:
  0.0 0.0 copy-start.3
  0.0 0.0 copy-start.2
  0.0 1.1 %extend.1 = (f32[16,8192]{1,0:T(8,128)S(1)}, s32[1,256]{1,0:T(1,128)S(1)}) custom-call(f32[6,8192]{1,0:T(8,128)} %coords_ref.1, f32[8,8192]{1,0:T(8,128)} %right_ref.1, s32[1,256]{1,0:T(1,128)} %index_hbm.1), custom_call_target="tpu_custom_call" | custom-call | tf_op jit(solution)/shard_map/extend/pallas_call | solution.py:112
  1.1 0.7 %collective-permute-start.1 = (f32[16,8192]{1,0:T(8,128)S(1)}, f32[16,8192]{1,0:T(8,128)S(1)}, u32[]{:S(2)}, u32[]{:S(2)}) collective-permute-start(f32[16,8192]{1,0:T(8,128)S(1)} %get-tuple-element.9.x_ref.own_ref), channel_id=1, source_target_pairs={{1,2},{2,1},{3,4},{4,3},{5,6},{6,5},{7,8},{8,7},{9,10},{10,9},{11,... | collective-permute-start | bytes 1572872 | tf_op jit(solution)/shard_map/ppermute | solution.py:28
  1.8 4.3 %collective-permute-start = (f32[16,8192]{1,0:T(8,128)S(1)}, f32[16,8192]{1,0:T(8,128)S(1)}, u32[]{:S(2)}, u32[]{:S(2)}) collective-permute-start(f32[16,8192]{1,0:T(8,128)S(1)} %get-tuple-element.9.x_ref.own_ref), channel_id=1, source_target_pairs={{0,1},{1,0},{2,3},{3,2},{4,5},{5,4},{6,7},{7,6},{8,9},{9,8},{10,11... | collective-permute-start | bytes 1572872 | tf_op jit(solution)/shard_map/ppermute | solution.py:28
  6.2 6.8 %first_step.1 = (f32[32,16,256]{2,1,0:T(8,128)}, f32[8,8192]{1,0:T(8,128)S(1)}) custom-call(f32[16,8192]{1,0:T(8,128)S(1)} %get-tuple-element.9.x_ref.own_ref, f32[8192,256]{1,0:T(8,128)} %proj_ref.1, s32[1,256]{1,0:T(1,128)S(1)} %get-tuple-element.10.index_ref), custom_call_target="tpu_custom_call" | custom-call | tf_op jit(solution)/shard_map/first_step/pallas_call | solution.py:171
  13.0 4.9 %all-to-all-start = ((f32[32,16,256]{2,1,0:T(8,128)}), f32[32,16,256]{2,1,0:T(8,128)S(1)}, u32[]{:S(2)}, u32[]{:S(2)}) async-start(f32[32,16,256]{2,1,0:T(8,128)} %get-tuple-element.12), calls=%async_computation | async-start | bytes 1048576 | tf_op jit(solution)/shard_map/all_to_all | solution.py:362
  17.9 0.0 copy-done.3
  17.9 0.1 copy.9.near_ref
  18.0 0.0 collective-permute-done.1.other_ref
  18.0 0.0 collective-permute-done.chip_ref
  18.0 0.0 copy-done.2
  18.0 0.0 copy-start
  18.0 0.0 copy-start.1
  18.1 19.1 %near_term.1.near_ref = f32[8,8192]{1,0:T(8,128)S(1)} custom-call(s32[32,8]{1,0:T(8,128)S(1)} %copy.9.near_ref, s32[32]{0:T(128)S(1)} %copy-done.2, f32[8,8192]{1,0:T(8,128)S(1)} %get-tuple-element.11.self_ref, f32[16,8192]{1,0:T(8,128)S(1)} %collective-permute-done.chip_ref, f32[16,8192]{1,0:T(8,128)S(1)} %get-tuple-element.9.x_ref.own_ref, ...), custom_call_target="tpu_custom_call" | custom-call | flops 16777216000 | bytes 2097152 | tf_op jit(solution)/shard_map/near_term/pallas_call | solution.py:288
  37.2 0.0 all-to-all-done.gathered_ref
  37.2 0.0 copy-done
  37.2 0.0 copy-done.1
  37.2 15.1 %far_term.1 = f32[8,8192]{1,0:T(8,128)} custom-call(f32[16,8192]{1,0:T(8,128)S(1)} %get-tuple-element.9.x_ref.own_ref, f32[8,8192]{1,0:T(8,128)S(1)} %near_term.1.near_ref, f32[32,16,256]{2,1,0:T(8,128)S(1)} %all-to-all-done.gathered_ref, s32[30,256]{1,0:T(8,128)S(1)} %copy-done.1, f32[512,256]{1,0:T(8,128)S(1)} %copy-done), custom_call_target="tpu_custom_call" | custom-call | tf_op jit(solution)/shard_map/far_term/pallas_call | solution.py:338
Async XLA Ops:
  0.0 17.9 %copy-start.3 = (s32[32,8]{0,1:T(8,128)S(1)}, s32[32,8]{0,1:T(8,128)}, u32[]{:S(2)}) copy-start(s32[32,8]{0,1:T(8,128)} %param.14) | copy-start | bytes 3076
  0.0 18.0 %copy-start.2 = (s32[32]{0:T(128)S(1)}, s32[32]{0:T(128)}, u32[]{:S(2)}) copy-start(s32[32]{0:T(128)} %count_ref.1) | copy-start | bytes 388
  1.1 16.9 %collective-permute-start.1 = (f32[16,8192]{1,0:T(8,128)S(1)}, f32[16,8192]{1,0:T(8,128)S(1)}, u32[]{:S(2)}, u32[]{:S(2)}) collective-permute-start(f32[16,8192]{1,0:T(8,128)S(1)} %get-tuple-element.9.x_ref.own_ref), channel_id=1, source_target_pairs={{1,2},{2,1},{3,4},{4,3},{5,6},{6,5},{7,8},{8,7},{9,10},{10,9},{11,... | collective-permute-start | bytes 1572872 | tf_op jit(solution)/shard_map/ppermute | solution.py:28
  1.8 16.2 %collective-permute-start = (f32[16,8192]{1,0:T(8,128)S(1)}, f32[16,8192]{1,0:T(8,128)S(1)}, u32[]{:S(2)}, u32[]{:S(2)}) collective-permute-start(f32[16,8192]{1,0:T(8,128)S(1)} %get-tuple-element.9.x_ref.own_ref), channel_id=1, source_target_pairs={{0,1},{1,0},{2,3},{3,2},{4,5},{5,4},{6,7},{7,6},{8,9},{9,8},{10,11... | collective-permute-start | bytes 1572872 | tf_op jit(solution)/shard_map/ppermute | solution.py:28
  13.0 24.2 %all-to-all-start = ((f32[32,16,256]{2,1,0:T(8,128)}), f32[32,16,256]{2,1,0:T(8,128)S(1)}, u32[]{:S(2)}, u32[]{:S(2)}) async-start(f32[32,16,256]{2,1,0:T(8,128)} %get-tuple-element.12), calls=%async_computation | async-start | bytes 1048576 | tf_op jit(solution)/shard_map/all_to_all | solution.py:362
  18.0 19.2 %copy-start = (f32[512,256]{1,0:T(8,128)S(1)}, f32[512,256]{1,0:T(8,128)}, u32[]{:S(2)}) copy-start(f32[512,256]{1,0:T(8,128)} %transfer_ref.1) | copy-start | bytes 1572868
  18.0 19.2 %copy-start.1 = (s32[30,256]{1,0:T(8,128)S(1)}, s32[30,256]{1,0:T(8,128)}, u32[]{:S(2)}) copy-start(s32[30,256]{1,0:T(8,128)} %selection_ref.1) | copy-start | bytes 92164
where the time goes:
time: 52.6 us; the launch traced here: 52.3 us
  Pallas kernels  42.1 us (80%)
  starting transfers between devices  9.96 us (19%)
    pallas_call x1, Pallas kernels, near_term(): pl.pallas_call(near_kernel, out_shape=jax.ShapeDtypeStruct((8, points), F...  19.1 us
    pallas_call x1, Pallas kernels, far_term(): pl.pallas_call(functools.partial(far_kernel, scale, tile), out_shape=jax....  15.1 us
    pallas_call x1, Pallas kernels, first_step(): pl.pallas_call(functools.partial(first_kernel, leaf), out_shape=(jax.Shap...  6.81 us
    ppermute x2, starting transfers between devices, swap(): return lax.ppermute(value, axis, pairs)  5.03 us
    all_to_all x1, starting transfers between devices, body(): gathered = lax.all_to_all(node, 'leaf', 0, 0, tiled=True)  4.93 us
    pallas_call x1, Pallas kernels, extend(): pl.pallas_call(extend_kernel, out_shape=(pltpu.VMEM((16, points), F32), p...  1.12 us
  transfers between devices with their start and end apart: 3, of which 0 were waited for; matrix products, arithmetic and copies ran while one was open for 0% of the time, Pallas kernels for 50%

commit v1 on v0

--- a/solution.py
+++ b/solution.py
@@ -12,8 +12,8 @@
 BF16 = jnp.bfloat16
 LANES = 128
 SHIFT = 2.0
-LEAVES_TURN = 4
-LEAVES_SELF = 8
+LEAVES_TURN = 8
+LEAVES_SELF = 16
 ROOT = math.sqrt(math.log2(math.e))
 SMEM_SPEC = pl.BlockSpec(memory_space=pltpu.SMEM)
 HBM_SPEC = pl.BlockSpec(memory_space=pltpu.HBM)
@@ -68,8 +68,8 @@
 
 
 def split_block(exponent):
-    kernel = jnp.exp2(exponent)
-    high = jnp.minimum(kernel.astype(BF16), jnp.ones((), BF16))
+    kernel = jnp.exp2(jnp.minimum(exponent, 0.0))
+    high = kernel.astype(BF16)
     return high, (kernel - high.astype(F32)).astype(BF16)
 
 

time: 52.6 us -> 50.2 us (0.954)
  Pallas kernels: 42.1 us -> 39.1 us
    pallas_call x1, Pallas kernels: 19.1 us -> 17.9 us  [near_term(): pl.pallas_call(near_kernel, out_shape=jax.ShapeDtypeStruct((8, points), F...]
    pallas_call x1, Pallas kernels: 15.1 us -> 13.9 us  [far_term(): pl.pallas_call(functools.partial(far_kernel, scale, tile), out_shape=jax....]
    pallas_call x1, Pallas kernels: 6.81 us -> 6.2 us  [first_step(): pl.pallas_call(functools.partial(first_kernel, leaf), out_shape=(jax.Shap...]
  transfers between devices with their start and end apart: 3 -> 3, of which waited for: 0 -> 0; matrix products, arithmetic and copies ran while one was open for 0% -> 0% of each run, Pallas kernels for 50% -> 49%
where the time goes in v1:
time: 50.2 us; the launch traced here: 49.5 us
  Pallas kernels  39.1 us (78%)
  starting transfers between devices  10.1 us (20%)
    pallas_call x1, Pallas kernels, near_term(): pl.pallas_call(near_kernel, out_shape=jax.ShapeDtypeStruct((8, points), F...  17.9 us
    pallas_call x1, Pallas kernels, far_term(): pl.pallas_call(functools.partial(far_kernel, scale, tile), out_shape=jax....  13.9 us
    pallas_call x1, Pallas kernels, first_step(): pl.pallas_call(functools.partial(first_kernel, leaf), out_shape=(jax.Shap...  6.2 us
    all_to_all x1, starting transfers between devices, body(): gathered = lax.all_to_all(node, 'leaf', 0, 0, tiled=True)  5.11 us
    ppermute x2, starting transfers between devices, swap(): return lax.ppermute(value, axis, pairs)  5.03 us
    pallas_call x1, Pallas kernels, extend(): pl.pallas_call(extend_kernel, out_shape=(pltpu.VMEM((16, points), F32), p...  1.12 us
  transfers between devices with their start and end apart: 3, of which 0 were waited for; matrix products, arithmetic and copies ran while one was open for 0% of the time, Pallas kernels for 49%

profile of v1, /device:TPU:0, one launch (start us, length us, event | category | flops | bytes accessed | tf_op | source)
XLA Modules:
  0.0 49.5 jit_solution(12235052583093772800)
XLA Ops:
  0.0 0.0 copy-start.3
  0.0 0.0 copy-start.2
  0.0 1.1 %extend.1 = (f32[16,8192]{1,0:T(8,128)S(1)}, s32[1,256]{1,0:T(1,128)S(1)}) custom-call(f32[6,8192]{1,0:T(8,128)} %coords_ref.1, f32[8,8192]{1,0:T(8,128)} %right_ref.1, s32[1,256]{1,0:T(1,128)} %index_hbm.1), custom_call_target="tpu_custom_call" | custom-call | tf_op jit(solution)/shard_map/extend/pallas_call | solution.py:112
  1.1 0.7 %collective-permute-start.1 = (f32[16,8192]{1,0:T(8,128)S(1)}, f32[16,8192]{1,0:T(8,128)S(1)}, u32[]{:S(2)}, u32[]{:S(2)}) collective-permute-start(f32[16,8192]{1,0:T(8,128)S(1)} %get-tuple-element.9.x_ref.own_ref), channel_id=1, source_target_pairs={{1,2},{2,1},{3,4},{4,3},{5,6},{6,5},{7,8},{8,7},{9,10},{10,9},{11,... | collective-permute-start | bytes 1572872 | tf_op jit(solution)/shard_map/ppermute | solution.py:28
  1.8 4.3 %collective-permute-start = (f32[16,8192]{1,0:T(8,128)S(1)}, f32[16,8192]{1,0:T(8,128)S(1)}, u32[]{:S(2)}, u32[]{:S(2)}) collective-permute-start(f32[16,8192]{1,0:T(8,128)S(1)} %get-tuple-element.9.x_ref.own_ref), channel_id=1, source_target_pairs={{0,1},{1,0},{2,3},{3,2},{4,5},{5,4},{6,7},{7,6},{8,9},{9,8},{10,11... | collective-permute-start | bytes 1572872 | tf_op jit(solution)/shard_map/ppermute | solution.py:28
  6.2 6.2 %first_step.1 = (f32[32,16,256]{2,1,0:T(8,128)}, f32[8,8192]{1,0:T(8,128)S(1)}) custom-call(f32[16,8192]{1,0:T(8,128)S(1)} %get-tuple-element.9.x_ref.own_ref, f32[8192,256]{1,0:T(8,128)} %proj_ref.1, s32[1,256]{1,0:T(1,128)S(1)} %get-tuple-element.10.index_ref), custom_call_target="tpu_custom_call" | custom-call | tf_op jit(solution)/shard_map/first_step/pallas_call | solution.py:171
  12.4 5.1 %all-to-all-start = ((f32[32,16,256]{2,1,0:T(8,128)}), f32[32,16,256]{2,1,0:T(8,128)S(1)}, u32[]{:S(2)}, u32[]{:S(2)}) async-start(f32[32,16,256]{2,1,0:T(8,128)} %get-tuple-element.12), calls=%async_computation | async-start | bytes 1048576 | tf_op jit(solution)/shard_map/all_to_all | solution.py:362
  17.5 0.0 copy-done.3
  17.5 0.1 copy.9.near_ref
  17.6 0.0 collective-permute-done.1.other_ref
  17.6 0.0 collective-permute-done.chip_ref
  17.6 0.0 copy-done.2
  17.6 0.0 copy-start
  17.6 0.0 copy-start.1
  17.6 17.9 %near_term.1.near_ref = f32[8,8192]{1,0:T(8,128)S(1)} custom-call(s32[32,8]{1,0:T(8,128)S(1)} %copy.9.near_ref, s32[32]{0:T(128)S(1)} %copy-done.2, f32[8,8192]{1,0:T(8,128)S(1)} %get-tuple-element.11.self_ref, f32[16,8192]{1,0:T(8,128)S(1)} %collective-permute-done.chip_ref, f32[16,8192]{1,0:T(8,128)S(1)} %get-tuple-element.9.x_ref.own_ref, ...), custom_call_target="tpu_custom_call" | custom-call | flops 16777216000 | bytes 2097152 | tf_op jit(solution)/shard_map/near_term/pallas_call | solution.py:288
  35.5 0.0 all-to-all-done.gathered_ref
  35.5 0.0 copy-done
  35.6 0.0 copy-done.1
  35.6 13.9 %far_term.1 = f32[8,8192]{1,0:T(8,128)} custom-call(f32[16,8192]{1,0:T(8,128)S(1)} %get-tuple-element.9.x_ref.own_ref, f32[8,8192]{1,0:T(8,128)S(1)} %near_term.1.near_ref, f32[32,16,256]{2,1,0:T(8,128)S(1)} %all-to-all-done.gathered_ref, s32[30,256]{1,0:T(8,128)S(1)} %copy-done.1, f32[512,256]{1,0:T(8,128)S(1)} %copy-done), custom_call_target="tpu_custom_call" | custom-call | tf_op jit(solution)/shard_map/far_term/pallas_call | solution.py:338
Async XLA Ops:
  0.0 17.5 %copy-start.3 = (s32[32,8]{0,1:T(8,128)S(1)}, s32[32,8]{0,1:T(8,128)}, u32[]{:S(2)}) copy-start(s32[32,8]{0,1:T(8,128)} %param.14) | copy-start | bytes 3076
  0.0 17.6 %copy-start.2 = (s32[32]{0:T(128)S(1)}, s32[32]{0:T(128)}, u32[]{:S(2)}) copy-start(s32[32]{0:T(128)} %count_ref.1) | copy-start | bytes 388
  1.1 16.5 %collective-permute-start.1 = (f32[16,8192]{1,0:T(8,128)S(1)}, f32[16,8192]{1,0:T(8,128)S(1)}, u32[]{:S(2)}, u32[]{:S(2)}) collective-permute-start(f32[16,8192]{1,0:T(8,128)S(1)} %get-tuple-element.9.x_ref.own_ref), channel_id=1, source_target_pairs={{1,2},{2,1},{3,4},{4,3},{5,6},{6,5},{7,8},{8,7},{9,10},{10,9},{11,... | collective-permute-start | bytes 1572872 | tf_op jit(solution)/shard_map/ppermute | solution.py:28
  1.8 15.8 %collective-permute-start = (f32[16,8192]{1,0:T(8,128)S(1)}, f32[16,8192]{1,0:T(8,128)S(1)}, u32[]{:S(2)}, u32[]{:S(2)}) collective-permute-start(f32[16,8192]{1,0:T(8,128)S(1)} %get-tuple-element.9.x_ref.own_ref), channel_id=1, source_target_pairs={{0,1},{1,0},{2,3},{3,2},{4,5},{5,4},{6,7},{7,6},{8,9},{9,8},{10,11... | collective-permute-start | bytes 1572872 | tf_op jit(solution)/shard_map/ppermute | solution.py:28
  12.4 23.2 %all-to-all-start = ((f32[32,16,256]{2,1,0:T(8,128)}), f32[32,16,256]{2,1,0:T(8,128)S(1)}, u32[]{:S(2)}, u32[]{:S(2)}) async-start(f32[32,16,256]{2,1,0:T(8,128)} %get-tuple-element.12), calls=%async_computation | async-start | bytes 1048576 | tf_op jit(solution)/shard_map/all_to_all | solution.py:362
  17.6 17.9 %copy-start = (f32[512,256]{1,0:T(8,128)S(1)}, f32[512,256]{1,0:T(8,128)}, u32[]{:S(2)}) copy-start(f32[512,256]{1,0:T(8,128)} %transfer_ref.1) | copy-start | bytes 1572868
  17.6 17.9 %copy-start.1 = (s32[30,256]{1,0:T(8,128)S(1)}, s32[30,256]{1,0:T(8,128)}, u32[]{:S(2)}) copy-start(s32[30,256]{1,0:T(8,128)} %selection_ref.1) | copy-start | bytes 92164

commit v2 on v1

--- a/solution.py
+++ b/solution.py
@@ -11,8 +11,9 @@
 F32 = jnp.float32
 BF16 = jnp.bfloat16
 LANES = 128
+ROWS = 32
 SHIFT = 2.0
-LEAVES_TURN = 8
+LEAVES_TURN = 16
 LEAVES_SELF = 16
 ROOT = math.sqrt(math.log2(math.e))
 SMEM_SPEC = pl.BlockSpec(memory_space=pltpu.SMEM)
@@ -33,23 +34,26 @@
     return high, value - high
 
 
-def three_pieces(value):
-    high, rest = two_pieces(value)
+def extended_pieces(extended):
+    high, rest = two_pieces(extended)
     middle, low = two_pieces(rest)
-    return high, middle, low
+    row = lax.broadcasted_iota(jnp.int32, extended.shape, 0)
+    return high, middle, jnp.where(row < 6, middle, low), row
 
 
 def source_form(extended):
-    high, middle, low = three_pieces(extended)
-    return jnp.concatenate([high, high, high, middle, middle, low], axis=0).astype(BF16)
+    high, middle, last, row = extended_pieces(extended)
+    last = jnp.where(row == 7, 1.0, last)
+    return jnp.concatenate([high, high, middle, last], axis=0).astype(BF16)
 
 
 def target_form(extended):
     row = lax.broadcasted_iota(jnp.int32, extended.shape, 0)
     below = pltpu.roll(extended, 1, 0)
     swapped = jnp.where(row == 6, 1.0, jnp.where(row == 7, below, extended))
-    high, middle, low = three_pieces(swapped)
-    return jnp.concatenate([high, middle, low, high, middle, high], axis=0).astype(BF16)
+    high, middle, last, _ = extended_pieces(swapped)
+    last = jnp.where(row == 6, 1.0, last)
+    return jnp.concatenate([high, middle, high, last], axis=0).astype(BF16)
 
 
 def weight_form(values):
@@ -73,16 +77,23 @@
     return high, (kernel - high.astype(F32)).astype(BF16)
 
 
-def kernel_term(source, target, weight, rows):
-    highs, lows = [], []
-    for first in range(0, source.shape[0], rows):
-        high, low = split_block(jnp.dot(source[first:first + rows], target, preferred_element_type=F32))
-        highs.append(high)
-        lows.append(low)
-    high = jnp.concatenate(highs, axis=0) if len(highs) > 1 else highs[0]
-    low = jnp.concatenate(lows, axis=0) if len(lows) > 1 else lows[0]
-    both = jnp.dot(weight, high, preferred_element_type=F32)
-    return both + jnp.dot(weight, low, preferred_element_type=F32)
+def repeat_blocks(weight):
+    pieces = []
+    for first in range(0, weight.shape[1], LANES):
+        pieces += [weight[:, first:first + LANES]] * 2
+    return jnp.concatenate(pieces, axis=1)
+
+
+def kernel_pieces(source, target):
+    pieces = []
+    for first in range(0, source.shape[0], LANES):
+        pieces += split_block(jnp.dot(source[first:first + LANES], target, preferred_element_type=F32))
+    return pieces
+
+
+def weigh(weights, pieces):
+    weights = jnp.concatenate(weights, axis=1) if len(weights) > 1 else weights[0]
+    return fold(jnp.dot(weights, jnp.concatenate(pieces, axis=0), preferred_element_type=F32))
 
 
 def fold(pieces):
@@ -140,14 +151,17 @@
     def prepare(at, _):
         columns = pl.ds(pl.multiple_of(at * wide, wide), wide)
         sources[:, columns] = source_form(x_ref[0:8, columns])
-        weights[:, columns] = weight_form(x_ref[8:16, columns])
+        twice = pl.ds(pl.multiple_of(at * 2 * wide, wide), 2 * wide)
+        weights[:, twice] = repeat_blocks(weight_form(x_ref[8:16, columns]))
         targets[:, columns] = target_form(x_ref[0:8, columns])
         return 0
 
     def turn(at, _):
         for part in range(LEAVES_SELF):
             columns = pl.ds(pl.multiple_of((at * LEAVES_SELF + part) * leaf, leaf), leaf)
-            self_ref[:, columns] = fold(kernel_term(sources[:, columns].T, targets[:, columns], weights[:, columns], 128))
+            twice = pl.ds(pl.multiple_of((at * LEAVES_SELF + part) * 2 * leaf, leaf), 2 * leaf)
+            pieces = kernel_pieces(sources[:, columns].T, targets[:, columns])
+            self_ref[:, columns] = weigh([weights[:, twice]], pieces)
         return 0
 
     lax.fori_loop(0, points // wide, prepare, 0)
@@ -178,9 +192,9 @@
         out_specs=(VMEM_SPEC, VMEM_SPEC),
         scratch_shapes=[
             pltpu.VMEM((chunks, points // chunks, rank), F32),
-            pltpu.VMEM((48, points), BF16),
-            pltpu.VMEM((16, points), BF16),
-            pltpu.VMEM((48, points), BF16),
+            pltpu.VMEM((ROWS, points), BF16),
+            pltpu.VMEM((16, 2 * points), BF16),
+            pltpu.VMEM((ROWS, points), BF16),
             pltpu.SemaphoreType.DMA((chunks,)),
         ],
         compiler_params=pltpu.CompilerParams(vmem_limit_bytes=50 * 2**20),
@@ -235,7 +249,8 @@
         for part, ref in enumerate((chip_ref, own_ref, other_ref)):
             window = pl.ds(pl.multiple_of(part * points + at * wide, wide), wide)
             sources[:, window] = source_form(ref[0:8, columns])
-            weights[:, window] = weight_form(ref[8:16, columns])
+            twice = pl.ds(pl.multiple_of(2 * (part * points + at * wide), wide), 2 * wide)
+            weights[:, twice] = repeat_blocks(weight_form(ref[8:16, columns]))
         targets[:, columns] = target_form(own_ref[0:8, columns])
         return 0
 
@@ -251,14 +266,14 @@
     def one_leaf(at, live_slots):
         columns = pl.ds(pl.multiple_of(at * leaf, leaf), leaf)
         target = targets[:, columns]
-        total = jnp.zeros((16, leaf), F32)
+        held, pieces = [], []
         for slot in range(1, live_slots):
             place = window_place(near_ref[at, slot] - first_leaf)
             window = pl.ds(pl.multiple_of(place * leaf, leaf), leaf)
-            weight = weights[:, window]
-            weight = jnp.where(slot < count_ref[at], weight, jnp.zeros_like(weight))
-            total += kernel_term(sources[:, window].T, target, weight, 128)
-        out_ref[:, columns] = self_ref[:, columns] + fold(total)
+            weight = weights[:, pl.ds(pl.multiple_of(place * 2 * leaf, leaf), 2 * leaf)]
+            held.append(jnp.where(slot < count_ref[at], weight, jnp.zeros_like(weight)))
+            pieces += kernel_pieces(sources[:, window].T, target)
+        out_ref[:, columns] = self_ref[:, columns] + weigh(held, pieces)
 
     def turn(at, _):
         most = count_ref[LEAVES_TURN * at]
@@ -291,9 +306,9 @@
         in_specs=[SMEM_SPEC] * 2 + [VMEM_SPEC] * 4,
         out_specs=VMEM_SPEC,
         scratch_shapes=[
-            pltpu.VMEM((48, 3 * points), BF16),
-            pltpu.VMEM((16, 3 * points), BF16),
-            pltpu.VMEM((48, points), BF16),
+            pltpu.VMEM((ROWS, 3 * points), BF16),
+            pltpu.VMEM((16, 6 * points), BF16),
+            pltpu.VMEM((ROWS, points), BF16),
         ],
         cost_estimate=pl.CostEstimate(flops=1000 * entries, bytes_accessed=4 * 64 * points, transcendentals=entries),
         compiler_params=pltpu.CompilerParams(vmem_limit_bytes=32 * 2**20),
@@ -311,8 +326,8 @@
     for level in range(levels):
         node = held[first + ((own_index >> level) ^ 1)]
         form = source_form(node[0:8])
-        sources[level] = jnp.concatenate([form, jnp.zeros((LANES - 48, rank), BF16)], axis=0).T
-        weights[level] = weight_form(node[8:16])
+        sources[level] = jnp.concatenate([form, jnp.zeros((LANES - ROWS, rank), BF16)], axis=0).T
+        weights[level] = repeat_blocks(weight_form(node[8:16]))
         if level < levels - 1:
             rows = devices - (devices >> level)
             climb(held, first, devices >> (level + 1), selection_ref, rows, transfer, nodes, rows)
@@ -322,11 +337,12 @@
         for part in range(LEAVES_TURN):
             columns = pl.ds(pl.multiple_of((at * LEAVES_TURN + part) * tile, tile), tile)
             target = target_form(own_ref[0:8, columns])
-            target = jnp.concatenate([target, jnp.zeros((LANES - 48, tile), BF16)], axis=0)
-            total = jnp.zeros((16, tile), F32)
+            target = jnp.concatenate([target, jnp.zeros((LANES - ROWS, tile), BF16)], axis=0)
+            pieces = []
             for level in range(levels):
-                total += kernel_term(sources[level], target, weights[level], rank)
-            out_ref[:, columns] = (fold(total) + near_ref[:, columns]) * scale
+                pieces += kernel_pieces(sources[level], target)
+            total = weigh([weights[level] for level in range(levels)], pieces)
+            out_ref[:, columns] = (total + near_ref[:, columns]) * scale
         return 0
 
     lax.fori_loop(0, own_ref.shape[1] // (tile * LEAVES_TURN), turn, 0)
@@ -343,7 +359,7 @@
         scratch_shapes=[
             pltpu.VMEM((devices - 2, 16, rank), F32),
             pltpu.VMEM((levels, rank, LANES), BF16),
-            pltpu.VMEM((levels, 16, rank), BF16),
+            pltpu.VMEM((levels, 16, 2 * rank), BF16),
         ],
         compiler_params=pltpu.CompilerParams(vmem_limit_bytes=32 * 2**20),
         name="far_term",

time: 50.2 us -> 49.1 us (0.978)
  Pallas kernels: 39.1 us -> 38.4 us
    pallas_call x1, Pallas kernels: 13.9 us -> 13.3 us  [far_term(): pl.pallas_call(functools.partial(far_kernel, scale, tile), out_shape=jax....]
where the time goes in v2:
time: 49.1 us; the launch traced here: 48.7 us
  Pallas kernels  38.4 us (78%)
  starting transfers between devices  10.1 us (21%)
    pallas_call x1, Pallas kernels, near_term(): pl.pallas_call(near_kernel, out_shape=jax.ShapeDtypeStruct((8, points), F...  17.4 us
    pallas_call x1, Pallas kernels, far_term(): pl.pallas_call(functools.partial(far_kernel, scale, tile), out_shape=jax....  13.3 us
    pallas_call x1, Pallas kernels, first_step(): pl.pallas_call(functools.partial(first_kernel, leaf), out_shape=(jax.Shap...  6.51 us
    all_to_all x1, starting transfers between devices, body(): gathered = lax.all_to_all(node, 'leaf', 0, 0, tiled=True)  5.11 us
    ppermute x2, starting transfers between devices, swap(): return lax.ppermute(value, axis, pairs)  5.03 us
    pallas_call x1, Pallas kernels, extend(): pl.pallas_call(extend_kernel, out_shape=(pltpu.VMEM((16, points), F32), p...  1.12 us
  transfers between devices with their start and end apart: 3, of which 0 were waited for; matrix products, arithmetic and copies ran while one was open for 0% of the time, Pallas kernels for 49%

profile of v2, /device:TPU:0, one launch (start us, length us, event | category | flops | bytes accessed | tf_op | source)
XLA Modules:
  0.0 48.7 jit_solution(11182636484935192486)
XLA Ops:
  0.0 0.0 copy-start.3
  0.0 0.0 copy-start.2
  0.0 1.1 %extend.1 = (f32[16,8192]{1,0:T(8,128)S(1)}, s32[1,256]{1,0:T(1,128)S(1)}) custom-call(f32[6,8192]{1,0:T(8,128)} %coords_ref.1, f32[8,8192]{1,0:T(8,128)} %right_ref.1, s32[1,256]{1,0:T(1,128)} %index_hbm.1), custom_call_target="tpu_custom_call" | custom-call | tf_op jit(solution)/shard_map/extend/pallas_call | solution.py:123
  1.1 0.7 %collective-permute-start.1 = (f32[16,8192]{1,0:T(8,128)S(1)}, f32[16,8192]{1,0:T(8,128)S(1)}, u32[]{:S(2)}, u32[]{:S(2)}) collective-permute-start(f32[16,8192]{1,0:T(8,128)S(1)} %get-tuple-element.9.x_ref.own_ref), channel_id=1, source_target_pairs={{1,2},{2,1},{3,4},{4,3},{5,6},{6,5},{7,8},{8,7},{9,10},{10,9},{11,... | collective-permute-start | bytes 1572872 | tf_op jit(solution)/shard_map/ppermute | solution.py:29
  1.8 4.3 %collective-permute-start = (f32[16,8192]{1,0:T(8,128)S(1)}, f32[16,8192]{1,0:T(8,128)S(1)}, u32[]{:S(2)}, u32[]{:S(2)}) collective-permute-start(f32[16,8192]{1,0:T(8,128)S(1)} %get-tuple-element.9.x_ref.own_ref), channel_id=1, source_target_pairs={{0,1},{1,0},{2,3},{3,2},{4,5},{5,4},{6,7},{7,6},{8,9},{9,8},{10,11... | collective-permute-start | bytes 1572872 | tf_op jit(solution)/shard_map/ppermute | solution.py:29
  6.2 6.5 %first_step.1 = (f32[32,16,256]{2,1,0:T(8,128)}, f32[8,8192]{1,0:T(8,128)S(1)}) custom-call(f32[16,8192]{1,0:T(8,128)S(1)} %get-tuple-element.9.x_ref.own_ref, f32[8192,256]{1,0:T(8,128)} %proj_ref.1, s32[1,256]{1,0:T(1,128)S(1)} %get-tuple-element.10.index_ref), custom_call_target="tpu_custom_call" | custom-call | tf_op jit(solution)/shard_map/first_step/pallas_call | solution.py:185
  12.7 5.1 %all-to-all-start = ((f32[32,16,256]{2,1,0:T(8,128)}), f32[32,16,256]{2,1,0:T(8,128)S(1)}, u32[]{:S(2)}, u32[]{:S(2)}) async-start(f32[32,16,256]{2,1,0:T(8,128)} %get-tuple-element.12), calls=%async_computation | async-start | bytes 1048576 | tf_op jit(solution)/shard_map/all_to_all | solution.py:378
  17.8 0.0 copy-done.3
  17.8 0.1 copy.9.near_ref
  17.9 0.0 collective-permute-done.1.other_ref
  17.9 0.0 collective-permute-done.chip_ref
  17.9 0.0 copy-done.2
  17.9 0.0 copy-start
  17.9 0.0 copy-start.1
  17.9 17.4 %near_term.1.near_ref = f32[8,8192]{1,0:T(8,128)S(1)} custom-call(s32[32,8]{1,0:T(8,128)S(1)} %copy.9.near_ref, s32[32]{0:T(128)S(1)} %copy-done.2, f32[8,8192]{1,0:T(8,128)S(1)} %get-tuple-element.11.self_ref, f32[16,8192]{1,0:T(8,128)S(1)} %collective-permute-done.chip_ref, f32[16,8192]{1,0:T(8,128)S(1)} %get-tuple-element.9.x_ref.own_ref, ...), custom_call_target="tpu_custom_call" | custom-call | flops 16777216000 | bytes 2097152 | tf_op jit(solution)/shard_map/near_term/pallas_call | solution.py:303
  35.4 0.0 all-to-all-done.gathered_ref
  35.4 0.0 copy-done
  35.4 0.0 copy-done.1
  35.4 13.3 %far_term.1 = f32[8,8192]{1,0:T(8,128)} custom-call(f32[16,8192]{1,0:T(8,128)S(1)} %get-tuple-element.9.x_ref.own_ref, f32[8,8192]{1,0:T(8,128)S(1)} %near_term.1.near_ref, f32[32,16,256]{2,1,0:T(8,128)S(1)} %all-to-all-done.gathered_ref, s32[30,256]{1,0:T(8,128)S(1)} %copy-done.1, f32[512,256]{1,0:T(8,128)S(1)} %copy-done), custom_call_target="tpu_custom_call" | custom-call | tf_op jit(solution)/shard_map/far_term/pallas_call | solution.py:354
Async XLA Ops:
  0.0 17.8 %copy-start.3 = (s32[32,8]{0,1:T(8,128)S(1)}, s32[32,8]{0,1:T(8,128)}, u32[]{:S(2)}) copy-start(s32[32,8]{0,1:T(8,128)} %param.14) | copy-start | bytes 3076
  0.0 17.9 %copy-start.2 = (s32[32]{0:T(128)S(1)}, s32[32]{0:T(128)}, u32[]{:S(2)}) copy-start(s32[32]{0:T(128)} %count_ref.1) | copy-start | bytes 388
  1.1 16.8 %collective-permute-start.1 = (f32[16,8192]{1,0:T(8,128)S(1)}, f32[16,8192]{1,0:T(8,128)S(1)}, u32[]{:S(2)}, u32[]{:S(2)}) collective-permute-start(f32[16,8192]{1,0:T(8,128)S(1)} %get-tuple-element.9.x_ref.own_ref), channel_id=1, source_target_pairs={{1,2},{2,1},{3,4},{4,3},{5,6},{6,5},{7,8},{8,7},{9,10},{10,9},{11,... | collective-permute-start | bytes 1572872 | tf_op jit(solution)/shard_map/ppermute | solution.py:29
  1.8 16.1 %collective-permute-start = (f32[16,8192]{1,0:T(8,128)S(1)}, f32[16,8192]{1,0:T(8,128)S(1)}, u32[]{:S(2)}, u32[]{:S(2)}) collective-permute-start(f32[16,8192]{1,0:T(8,128)S(1)} %get-tuple-element.9.x_ref.own_ref), channel_id=1, source_target_pairs={{0,1},{1,0},{2,3},{3,2},{4,5},{5,4},{6,7},{7,6},{8,9},{9,8},{10,11... | collective-permute-start | bytes 1572872 | tf_op jit(solution)/shard_map/ppermute | solution.py:29
  12.7 22.7 %all-to-all-start = ((f32[32,16,256]{2,1,0:T(8,128)}), f32[32,16,256]{2,1,0:T(8,128)S(1)}, u32[]{:S(2)}, u32[]{:S(2)}) async-start(f32[32,16,256]{2,1,0:T(8,128)} %get-tuple-element.12), calls=%async_computation | async-start | bytes 1048576 | tf_op jit(solution)/shard_map/all_to_all | solution.py:378
  17.9 17.5 %copy-start = (f32[512,256]{1,0:T(8,128)S(1)}, f32[512,256]{1,0:T(8,128)}, u32[]{:S(2)}) copy-start(f32[512,256]{1,0:T(8,128)} %transfer_ref.1) | copy-start | bytes 1572868
  17.9 17.5 %copy-start.1 = (s32[30,256]{1,0:T(8,128)S(1)}, s32[30,256]{1,0:T(8,128)}, u32[]{:S(2)}) copy-start(s32[30,256]{1,0:T(8,128)} %selection_ref.1) | copy-start | bytes 92164

commit v3 on v2

--- a/solution.py
+++ b/solution.py
@@ -11,9 +11,9 @@
 F32 = jnp.float32
 BF16 = jnp.bfloat16
 LANES = 128
-ROWS = 32
 SHIFT = 2.0
-LEAVES_TURN = 16
+NEAR_TURN = 16
+FAR_TURN = 32
 LEAVES_SELF = 16
 ROOT = math.sqrt(math.log2(math.e))
 SMEM_SPEC = pl.BlockSpec(memory_space=pltpu.SMEM)
@@ -34,26 +34,23 @@
     return high, value - high
 
 
-def extended_pieces(extended):
-    high, rest = two_pieces(extended)
+def three_pieces(value):
+    high, rest = two_pieces(value)
     middle, low = two_pieces(rest)
-    row = lax.broadcasted_iota(jnp.int32, extended.shape, 0)
-    return high, middle, jnp.where(row < 6, middle, low), row
+    return high, middle, low
 
 
 def source_form(extended):
-    high, middle, last, row = extended_pieces(extended)
-    last = jnp.where(row == 7, 1.0, last)
-    return jnp.concatenate([high, high, middle, last], axis=0).astype(BF16)
+    high, middle, low = three_pieces(extended)
+    return jnp.concatenate([high, high, high, middle, middle, low], axis=0).astype(BF16)
 
 
 def target_form(extended):
     row = lax.broadcasted_iota(jnp.int32, extended.shape, 0)
     below = pltpu.roll(extended, 1, 0)
     swapped = jnp.where(row == 6, 1.0, jnp.where(row == 7, below, extended))
-    high, middle, last, _ = extended_pieces(swapped)
-    last = jnp.where(row == 6, 1.0, last)
-    return jnp.concatenate([high, middle, high, last], axis=0).astype(BF16)
+    high, middle, low = three_pieces(swapped)
+    return jnp.concatenate([high, middle, low, high, middle, high], axis=0).astype(BF16)
 
 
 def weight_form(values):
@@ -84,6 +81,16 @@
     return jnp.concatenate(pieces, axis=1)
 
 
+def kernel_term(source, target, weight):
+    total = None
+    for first in range(0, source.shape[0], LANES):
+        high, low = split_block(jnp.dot(source[first:first + LANES], target, preferred_element_type=F32))
+        both = jnp.concatenate([high, low], axis=0)
+        term = jnp.dot(weight[:, 2 * first:2 * (first + LANES)], both, preferred_element_type=F32)
+        total = term if total is None else total + term
+    return total
+
+
 def kernel_pieces(source, target):
     pieces = []
     for first in range(0, source.shape[0], LANES):
@@ -92,7 +99,7 @@
 
 
 def weigh(weights, pieces):
-    weights = jnp.concatenate(weights, axis=1) if len(weights) > 1 else weights[0]
+    weights = jnp.concatenate(weights, axis=1)
     return fold(jnp.dot(weights, jnp.concatenate(pieces, axis=0), preferred_element_type=F32))
 
 
@@ -146,7 +153,7 @@
         columns = pick_columns(pieces, index_ref[:, lanes])
         for copy in range(node_ref.shape[0]):
             node_ref[copy, 0:8, lanes] = columns
-    wide = 4 * leaf
+    wide = 8 * leaf
 
     def prepare(at, _):
         columns = pl.ds(pl.multiple_of(at * wide, wide), wide)
@@ -160,8 +167,7 @@
         for part in range(LEAVES_SELF):
             columns = pl.ds(pl.multiple_of((at * LEAVES_SELF + part) * leaf, leaf), leaf)
             twice = pl.ds(pl.multiple_of((at * LEAVES_SELF + part) * 2 * leaf, leaf), 2 * leaf)
-            pieces = kernel_pieces(sources[:, columns].T, targets[:, columns])
-            self_ref[:, columns] = weigh([weights[:, twice]], pieces)
+            self_ref[:, columns] = fold(kernel_term(sources[:, columns].T, targets[:, columns], weights[:, twice]))
         return 0
 
     lax.fori_loop(0, points // wide, prepare, 0)
@@ -192,9 +198,9 @@
         out_specs=(VMEM_SPEC, VMEM_SPEC),
         scratch_shapes=[
             pltpu.VMEM((chunks, points // chunks, rank), F32),
-            pltpu.VMEM((ROWS, points), BF16),
+            pltpu.VMEM((48, points), BF16),
             pltpu.VMEM((16, 2 * points), BF16),
-            pltpu.VMEM((ROWS, points), BF16),
+            pltpu.VMEM((48, points), BF16),
             pltpu.SemaphoreType.DMA((chunks,)),
         ],
         compiler_params=pltpu.CompilerParams(vmem_limit_bytes=50 * 2**20),
@@ -242,7 +248,7 @@
     own_index = lax.axis_index("leaf")
     even = own_index % 2 == 0
     first_leaf = own_index * leaves
-    wide = 4 * leaf
+    wide = 8 * leaf
 
     def prepare(at, _):
         columns = pl.ds(pl.multiple_of(at * wide, wide), wide)
@@ -276,24 +282,24 @@
         out_ref[:, columns] = self_ref[:, columns] + weigh(held, pieces)
 
     def turn(at, _):
-        most = count_ref[LEAVES_TURN * at]
-        for leaf_at in range(1, LEAVES_TURN):
-            most = jnp.maximum(most, count_ref[LEAVES_TURN * at + leaf_at])
+        most = count_ref[NEAR_TURN * at]
+        for leaf_at in range(1, NEAR_TURN):
+            most = jnp.maximum(most, count_ref[NEAR_TURN * at + leaf_at])
         heavy = most > slots // 2
 
         @pl.when(heavy)
         def _():
-            for leaf_at in range(LEAVES_TURN):
-                one_leaf(LEAVES_TURN * at + leaf_at, slots)
+            for leaf_at in range(NEAR_TURN):
+                one_leaf(NEAR_TURN * at + leaf_at, slots)
 
         @pl.when(jnp.logical_not(heavy))
         def _():
-            for leaf_at in range(LEAVES_TURN):
-                one_leaf(LEAVES_TURN * at + leaf_at, slots // 2)
+            for leaf_at in range(NEAR_TURN):
+                one_leaf(NEAR_TURN * at + leaf_at, slots // 2)
 
         return 0
 
-    lax.fori_loop(0, leaves // LEAVES_TURN, turn, 0)
+    lax.fori_loop(0, leaves // NEAR_TURN, turn, 0)
 
 
 def near_term(near_leaf, near_count, own_part, chip, own, other):
@@ -306,9 +312,9 @@
         in_specs=[SMEM_SPEC] * 2 + [VMEM_SPEC] * 4,
         out_specs=VMEM_SPEC,
         scratch_shapes=[
-            pltpu.VMEM((ROWS, 3 * points), BF16),
+            pltpu.VMEM((48, 3 * points), BF16),
             pltpu.VMEM((16, 6 * points), BF16),
-            pltpu.VMEM((ROWS, points), BF16),
+            pltpu.VMEM((48, points), BF16),
         ],
         cost_estimate=pl.CostEstimate(flops=1000 * entries, bytes_accessed=4 * 64 * points, transcendentals=entries),
         compiler_params=pltpu.CompilerParams(vmem_limit_bytes=32 * 2**20),
@@ -326,7 +332,7 @@
     for level in range(levels):
         node = held[first + ((own_index >> level) ^ 1)]
         form = source_form(node[0:8])
-        sources[level] = jnp.concatenate([form, jnp.zeros((LANES - ROWS, rank), BF16)], axis=0).T
+        sources[level] = jnp.concatenate([form, jnp.zeros((LANES - 48, rank), BF16)], axis=0).T
         weights[level] = repeat_blocks(weight_form(node[8:16]))
         if level < levels - 1:
             rows = devices - (devices >> level)
@@ -334,10 +340,10 @@
             held, first = nodes, rows
 
     def turn(at, _):
-        for part in range(LEAVES_TURN):
-            columns = pl.ds(pl.multiple_of((at * LEAVES_TURN + part) * tile, tile), tile)
+        for part in range(FAR_TURN):
+            columns = pl.ds(pl.multiple_of((at * FAR_TURN + part) * tile, tile), tile)
             target = target_form(own_ref[0:8, columns])
-            target = jnp.concatenate([target, jnp.zeros((LANES - ROWS, tile), BF16)], axis=0)
+            target = jnp.concatenate([target, jnp.zeros((LANES - 48, tile), BF16)], axis=0)
             pieces = []
             for level in range(levels):
                 pieces += kernel_pieces(sources[level], target)
@@ -345,7 +351,7 @@
             out_ref[:, columns] = (total + near_ref[:, columns]) * scale
         return 0
 
-    lax.fori_loop(0, own_ref.shape[1] // (tile * LEAVES_TURN), turn, 0)
+    lax.fori_loop(0, own_ref.shape[1] // (tile * FAR_TURN), turn, 0)
 
 
 def far_term(scale, tile, own, near, gathered, selection, transfer):

time: 49.1 us -> 48 us (0.978)
  Pallas kernels: 38.4 us -> 37.2 us
    pallas_call x1, Pallas kernels: 13.3 us -> 12.5 us  [far_term(): pl.pallas_call(functools.partial(far_kernel, scale, tile), out_shape=jax....]
  transfers between devices with their start and end apart: 3 -> 3, of which waited for: 0 -> 0; matrix products, arithmetic and copies ran while one was open for 0% -> 0% of each run, Pallas kernels for 49% -> 50%
where the time goes in v3:
time: 48 us; the launch traced here: 47.5 us
  Pallas kernels  37.2 us (78%)
  starting transfers between devices  10.1 us (21%)
    pallas_call x1, Pallas kernels, near_term(): pl.pallas_call(near_kernel, out_shape=jax.ShapeDtypeStruct((8, points), F...  17.3 us
    pallas_call x1, Pallas kernels, far_term(): pl.pallas_call(functools.partial(far_kernel, scale, tile), out_shape=jax....  12.5 us
    pallas_call x1, Pallas kernels, first_step(): pl.pallas_call(functools.partial(first_kernel, leaf), out_shape=(jax.Shap...  6.19 us
    all_to_all x1, starting transfers between devices, body(): gathered = lax.all_to_all(node, 'leaf', 0, 0, tiled=True)  5.11 us
    ppermute x2, starting transfers between devices, swap(): return lax.ppermute(value, axis, pairs)  5.03 us
    pallas_call x1, Pallas kernels, extend(): pl.pallas_call(extend_kernel, out_shape=(pltpu.VMEM((16, points), F32), p...  1.12 us
  transfers between devices with their start and end apart: 3, of which 0 were waited for; matrix products, arithmetic and copies ran while one was open for 0% of the time, Pallas kernels for 50%

profile of v3, /device:TPU:0, one launch (start us, length us, event | category | flops | bytes accessed | tf_op | source)
XLA Modules:
  0.0 47.5 jit_solution(18030949033503224210)
XLA Ops:
  0.0 0.0 copy-start.3
  0.0 0.0 copy-start.2
  0.0 1.1 %extend.1 = (f32[16,8192]{1,0:T(8,128)S(1)}, s32[1,256]{1,0:T(1,128)S(1)}) custom-call(f32[6,8192]{1,0:T(8,128)} %coords_ref.1, f32[8,8192]{1,0:T(8,128)} %right_ref.1, s32[1,256]{1,0:T(1,128)} %index_hbm.1), custom_call_target="tpu_custom_call" | custom-call | tf_op jit(solution)/shard_map/extend/pallas_call | solution.py:130
  1.1 0.7 %collective-permute-start.1 = (f32[16,8192]{1,0:T(8,128)S(1)}, f32[16,8192]{1,0:T(8,128)S(1)}, u32[]{:S(2)}, u32[]{:S(2)}) collective-permute-start(f32[16,8192]{1,0:T(8,128)S(1)} %get-tuple-element.9.x_ref.own_ref), channel_id=1, source_target_pairs={{1,2},{2,1},{3,4},{4,3},{5,6},{6,5},{7,8},{8,7},{9,10},{10,9},{11,... | collective-permute-start | bytes 1572872 | tf_op jit(solution)/shard_map/ppermute | solution.py:29
  1.8 4.3 %collective-permute-start = (f32[16,8192]{1,0:T(8,128)S(1)}, f32[16,8192]{1,0:T(8,128)S(1)}, u32[]{:S(2)}, u32[]{:S(2)}) collective-permute-start(f32[16,8192]{1,0:T(8,128)S(1)} %get-tuple-element.9.x_ref.own_ref), channel_id=1, source_target_pairs={{0,1},{1,0},{2,3},{3,2},{4,5},{5,4},{6,7},{7,6},{8,9},{9,8},{10,11... | collective-permute-start | bytes 1572872 | tf_op jit(solution)/shard_map/ppermute | solution.py:29
  6.2 6.2 %first_step.1 = (f32[32,16,256]{2,1,0:T(8,128)}, f32[8,8192]{1,0:T(8,128)S(1)}) custom-call(f32[16,8192]{1,0:T(8,128)S(1)} %get-tuple-element.9.x_ref.own_ref, f32[8192,256]{1,0:T(8,128)} %proj_ref.1, s32[1,256]{1,0:T(1,128)S(1)} %get-tuple-element.10.index_ref), custom_call_target="tpu_custom_call" | custom-call | tf_op jit(solution)/shard_map/first_step/pallas_call | solution.py:191
  12.4 5.1 %all-to-all-start = ((f32[32,16,256]{2,1,0:T(8,128)}), f32[32,16,256]{2,1,0:T(8,128)S(1)}, u32[]{:S(2)}, u32[]{:S(2)}) async-start(f32[32,16,256]{2,1,0:T(8,128)} %get-tuple-element.12), calls=%async_computation | async-start | bytes 1048576 | tf_op jit(solution)/shard_map/all_to_all | solution.py:384
  17.5 0.0 copy-done.3
  17.5 0.1 copy.9.near_ref
  17.6 0.0 collective-permute-done.1.other_ref
  17.6 0.0 collective-permute-done.chip_ref
  17.6 0.0 copy-done.2
  17.6 0.0 copy-start
  17.6 0.0 copy-start.1
  17.6 17.3 %near_term.1.near_ref = f32[8,8192]{1,0:T(8,128)S(1)} custom-call(s32[32,8]{1,0:T(8,128)S(1)} %copy.9.near_ref, s32[32]{0:T(128)S(1)} %copy-done.2, f32[8,8192]{1,0:T(8,128)S(1)} %get-tuple-element.11.self_ref, f32[16,8192]{1,0:T(8,128)S(1)} %collective-permute-done.chip_ref, f32[16,8192]{1,0:T(8,128)S(1)} %get-tuple-element.9.x_ref.own_ref, ...), custom_call_target="tpu_custom_call" | custom-call | flops 16777216000 | bytes 2097152 | tf_op jit(solution)/shard_map/near_term/pallas_call | solution.py:309
  34.9 0.0 all-to-all-done.gathered_ref
  35.0 0.0 copy-done
  35.0 0.0 copy-done.1
  35.0 12.5 %far_term.1 = f32[8,8192]{1,0:T(8,128)} custom-call(f32[16,8192]{1,0:T(8,128)S(1)} %get-tuple-element.9.x_ref.own_ref, f32[8,8192]{1,0:T(8,128)S(1)} %near_term.1.near_ref, f32[32,16,256]{2,1,0:T(8,128)S(1)} %all-to-all-done.gathered_ref, s32[30,256]{1,0:T(8,128)S(1)} %copy-done.1, f32[512,256]{1,0:T(8,128)S(1)} %copy-done), custom_call_target="tpu_custom_call" | custom-call | tf_op jit(solution)/shard_map/far_term/pallas_call | solution.py:360
Async XLA Ops:
  0.0 17.5 %copy-start.3 = (s32[32,8]{0,1:T(8,128)S(1)}, s32[32,8]{0,1:T(8,128)}, u32[]{:S(2)}) copy-start(s32[32,8]{0,1:T(8,128)} %param.14) | copy-start | bytes 3076
  0.0 17.6 %copy-start.2 = (s32[32]{0:T(128)S(1)}, s32[32]{0:T(128)}, u32[]{:S(2)}) copy-start(s32[32]{0:T(128)} %count_ref.1) | copy-start | bytes 388
  1.1 16.4 %collective-permute-start.1 = (f32[16,8192]{1,0:T(8,128)S(1)}, f32[16,8192]{1,0:T(8,128)S(1)}, u32[]{:S(2)}, u32[]{:S(2)}) collective-permute-start(f32[16,8192]{1,0:T(8,128)S(1)} %get-tuple-element.9.x_ref.own_ref), channel_id=1, source_target_pairs={{1,2},{2,1},{3,4},{4,3},{5,6},{6,5},{7,8},{8,7},{9,10},{10,9},{11,... | collective-permute-start | bytes 1572872 | tf_op jit(solution)/shard_map/ppermute | solution.py:29
  1.8 15.7 %collective-permute-start = (f32[16,8192]{1,0:T(8,128)S(1)}, f32[16,8192]{1,0:T(8,128)S(1)}, u32[]{:S(2)}, u32[]{:S(2)}) collective-permute-start(f32[16,8192]{1,0:T(8,128)S(1)} %get-tuple-element.9.x_ref.own_ref), channel_id=1, source_target_pairs={{0,1},{1,0},{2,3},{3,2},{4,5},{5,4},{6,7},{7,6},{8,9},{9,8},{10,11... | collective-permute-start | bytes 1572872 | tf_op jit(solution)/shard_map/ppermute | solution.py:29
  12.4 22.6 %all-to-all-start = ((f32[32,16,256]{2,1,0:T(8,128)}), f32[32,16,256]{2,1,0:T(8,128)S(1)}, u32[]{:S(2)}, u32[]{:S(2)}) async-start(f32[32,16,256]{2,1,0:T(8,128)} %get-tuple-element.12), calls=%async_computation | async-start | bytes 1048576 | tf_op jit(solution)/shard_map/all_to_all | solution.py:384
  17.6 17.4 %copy-start = (f32[512,256]{1,0:T(8,128)S(1)}, f32[512,256]{1,0:T(8,128)}, u32[]{:S(2)}) copy-start(f32[512,256]{1,0:T(8,128)} %transfer_ref.1) | copy-start | bytes 1572868
  17.6 17.4 %copy-start.1 = (s32[30,256]{1,0:T(8,128)S(1)}, s32[30,256]{1,0:T(8,128)}, u32[]{:S(2)}) copy-start(s32[30,256]{1,0:T(8,128)} %selection_ref.1) | copy-start | bytes 92164

commit v4 on v3

--- a/solution.py
+++ b/solution.py
@@ -14,7 +14,7 @@
 SHIFT = 2.0
 NEAR_TURN = 16
 FAR_TURN = 32
-LEAVES_SELF = 16
+LEAVES_SELF = 32
 ROOT = math.sqrt(math.log2(math.e))
 SMEM_SPEC = pl.BlockSpec(memory_space=pltpu.SMEM)
 HBM_SPEC = pl.BlockSpec(memory_space=pltpu.HBM)
@@ -107,32 +107,55 @@
     return pieces[:8] + pieces[8:]
 
 
-def extend_kernel(coords_ref, right_ref, index_hbm, out_ref, index_ref, held, sems):
+def add_norm(ref):
+    centred = ref[0:6, :]
+    ref[6:7, :] = -0.5 * jnp.sum(centred * centred, axis=0, keepdims=True)
+    ref[7:8, :] = jnp.ones((1, centred.shape[1]), F32)
+
+
+def packed_parts(points):
+    quarter = points // 4
+    return slice(points, points + 3 * quarter), [
+        slice(points + part * quarter, points + (part + 1) * quarter) for part in range(3)
+    ]
+
+
+def extend_kernel(coords_ref, right_ref, index_hbm, out_ref, packed_ref, index_ref, held, sems):
     rows, points = held.shape
     copies = [
         pltpu.make_async_copy(coords_ref, held, sems.at[0]),
         pltpu.make_async_copy(right_ref, out_ref.at[pl.ds(8, 8)], sems.at[1]),
-        pltpu.make_async_copy(index_hbm, index_ref, sems.at[2]),
+        pltpu.make_async_copy(right_ref, packed_ref.at[:, pl.ds(0, points)], sems.at[2]),
+        pltpu.make_async_copy(index_hbm, index_ref, sems.at[3]),
     ]
     for copy in copies:
         copy.start()
     copies[0].wait()
     centred = (held[...] - SHIFT) * ROOT
     out_ref[0:rows, :] = centred
+    front, parts = packed_parts(points)
+    last = 3 * (points // 4)
+    packed_ref[0:rows, front] = centred[:, :last]
+    for part, columns in enumerate(parts):
+        packed_ref[rows:rows + 2, columns] = out_ref[2 * part:2 * part + 2, last:]
     out_ref[rows:rows + 1, :] = -0.5 * jnp.sum(centred * centred, axis=0, keepdims=True)
     out_ref[rows + 1:rows + 2, :] = jnp.ones((1, points), F32)
-    copies[1].wait()
-    copies[2].wait()
+    for copy in copies[1:]:
+        copy.wait()
 
 
 def extend(coords, right_sides, skel_index):
     rows, points = coords.shape
     return pl.pallas_call(
         extend_kernel,
-        out_shape=(pltpu.VMEM((16, points), F32), pltpu.VMEM(skel_index.shape, jnp.int32)),
+        out_shape=(
+            pltpu.VMEM((16, points), F32),
+            pltpu.VMEM((8, points + 3 * (points // 4)), F32),
+            pltpu.VMEM(skel_index.shape, jnp.int32),
+        ),
         in_specs=[HBM_SPEC] * 3,
-        out_specs=(VMEM_SPEC, VMEM_SPEC),
-        scratch_shapes=[pltpu.VMEM((rows, points), F32), pltpu.SemaphoreType.DMA((3,))],
+        out_specs=(VMEM_SPEC,) * 3,
+        scratch_shapes=[pltpu.VMEM((rows, points), F32), pltpu.SemaphoreType.DMA((4,))],
         compiler_params=pltpu.CompilerParams(vmem_limit_bytes=58 * 2**20),
         name="extend",
     )(coords, right_sides, skel_index)
@@ -241,7 +264,7 @@
     return t_high.astype(BF16), t_low.astype(BF16)
 
 
-def near_kernel(near_ref, count_ref, self_ref, chip_ref, own_ref, other_ref, out_ref, sources, weights, targets):
+def near_kernel(near_ref, count_ref, self_ref, chip_ref, own_ref, other_ref, out_ref, sources, weights, targets, unpacked):
     leaves, slots = near_ref.shape
     points = own_ref.shape[1]
     leaf = points // leaves
@@ -250,13 +273,24 @@
     first_leaf = own_index * leaves
     wide = 8 * leaf
 
+    front, parts = packed_parts(points)
+    last = 3 * (points // 4)
+    for side, ref in enumerate((chip_ref, other_ref)):
+        target = unpacked.at[side]
+        target[0:6, 0:last] = ref[0:6, front]
+        for part, columns in enumerate(parts):
+            target[2 * part:2 * part + 2, last:] = ref[6:8, columns]
+        add_norm(target)
+
     def prepare(at, _):
         columns = pl.ds(pl.multiple_of(at * wide, wide), wide)
-        for part, ref in enumerate((chip_ref, own_ref, other_ref)):
+        for part, (coords, values) in enumerate(
+            ((unpacked.at[0], chip_ref), (own_ref, own_ref.at[pl.ds(8, 8)]), (unpacked.at[1], other_ref))
+        ):
             window = pl.ds(pl.multiple_of(part * points + at * wide, wide), wide)
-            sources[:, window] = source_form(ref[0:8, columns])
+            sources[:, window] = source_form(coords[0:8, columns])
             twice = pl.ds(pl.multiple_of(2 * (part * points + at * wide), wide), 2 * wide)
-            weights[:, twice] = repeat_blocks(weight_form(ref[8:16, columns]))
+            weights[:, twice] = repeat_blocks(weight_form(values[0:8, columns]))
         targets[:, columns] = target_form(own_ref[0:8, columns])
         return 0
 
@@ -315,6 +349,7 @@
             pltpu.VMEM((48, 3 * points), BF16),
             pltpu.VMEM((16, 6 * points), BF16),
             pltpu.VMEM((48, points), BF16),
+            pltpu.VMEM((2, 8, points), F32),
         ],
         cost_estimate=pl.CostEstimate(flops=1000 * entries, bytes_accessed=4 * 64 * points, transcendentals=entries),
         compiler_params=pltpu.CompilerParams(vmem_limit_bytes=32 * 2**20),
@@ -377,9 +412,9 @@
     leaves, slots = near_leaf.shape
     leaf = coords.shape[1] // leaves
     scale = 1.0 / (slots * leaf) ** 0.5
-    extended, skel_index = extend(coords, right_sides, skel_index)
-    chip = swap(extended, "leaf", 0)
-    other = swap(extended, "leaf", 1)
+    extended, packed, skel_index = extend(coords, right_sides, skel_index)
+    chip = swap(packed, "leaf", 0)
+    other = swap(packed, "leaf", 1)
     node, own_part = first_step(devices, leaf, extended, projection, skel_index)
     gathered = lax.all_to_all(node, "leaf", 0, 0, tiled=True)
     near = near_term(near_leaf, near_count, own_part, chip, extended, other)

time: 48 us -> 51.6 us (1.075)
  Pallas kernels: 37.2 us -> 41.2 us
    pallas_call x1, Pallas kernels: 6.19 us -> 9.64 us  [first_step(): pl.pallas_call(functools.partial(first_kernel, leaf), out_shape=(jax.Shap...]
  transfers between devices with their start and end apart: 3 -> 3, of which waited for: 0 -> 0; matrix products, arithmetic and copies ran while one was open for 0% -> 0% of each run, Pallas kernels for 50% -> 53%
where the time goes in v4:
time: 51.6 us; the launch traced here: 51.3 us
  Pallas kernels  41.2 us (80%)
  starting transfers between devices  9.96 us (19%)
    pallas_call x1, Pallas kernels, near_term(): pl.pallas_call(near_kernel, out_shape=jax.ShapeDtypeStruct((8, points), F...  17.8 us
    pallas_call x1, Pallas kernels, far_term(): pl.pallas_call(functools.partial(far_kernel, scale, tile), out_shape=jax....  12.5 us
    pallas_call x1, Pallas kernels, first_step(): pl.pallas_call(functools.partial(first_kernel, leaf), out_shape=(jax.Shap...  9.64 us
    ppermute x2, starting transfers between devices, swap(): return lax.ppermute(value, axis, pairs)  5.03 us
    all_to_all x1, starting transfers between devices, body(): gathered = lax.all_to_all(node, 'leaf', 0, 0, tiled=True)  4.94 us
    pallas_call x1, Pallas kernels, extend(): pl.pallas_call(extend_kernel, out_shape=(pltpu.VMEM((16, points), F32), p...  1.2 us
  transfers between devices with their start and end apart: 3, of which 0 were waited for; matrix products, arithmetic and copies ran while one was open for 0% of the time, Pallas kernels for 53%

profile of v4, /device:TPU:0, one launch (start us, length us, event | category | flops | bytes accessed | tf_op | source)
XLA Modules:
  0.0 51.3 jit_solution(5595276341076228746)
XLA Ops:
  0.0 0.0 copy-start.3
  0.0 0.0 copy-start.2
  0.0 1.2 %extend.1 = (f32[16,8192]{1,0:T(8,128)S(1)}, f32[8,14336]{1,0:T(8,128)S(1)}, s32[1,256]{1,0:T(1,128)S(1)}) custom-call(f32[6,8192]{1,0:T(8,128)} %coords_ref.1, f32[8,8192]{1,0:T(8,128)} %right_ref.1, s32[1,256]{1,0:T(1,128)} %index_hbm.1), custom_call_target="tpu_custom_call" | custom-call | tf_op jit(solution)/shard_map/extend/pallas_call | solution.py:149
  1.2 0.7 %collective-permute-start.1 = (f32[8,14336]{1,0:T(8,128)S(1)}, f32[8,14336]{1,0:T(8,128)S(1)}, u32[]{:S(2)}, u32[]{:S(2)}) collective-permute-start(f32[8,14336]{1,0:T(8,128)S(1)} %get-tuple-element.13), channel_id=1, source_target_pairs={{1,2},{2,1},{3,4},{4,3},{5,6},{6,5},{7,8},{8,7},{9,10},{10,9},{11,... | collective-permute-start | bytes 1376264 | tf_op jit(solution)/shard_map/ppermute | solution.py:29
  1.9 4.3 %collective-permute-start = (f32[8,14336]{1,0:T(8,128)S(1)}, f32[8,14336]{1,0:T(8,128)S(1)}, u32[]{:S(2)}, u32[]{:S(2)}) collective-permute-start(f32[8,14336]{1,0:T(8,128)S(1)} %get-tuple-element.13), channel_id=1, source_target_pairs={{0,1},{1,0},{2,3},{3,2},{4,5},{5,4},{6,7},{7,6},{8,9},{9,8},{10,11... | collective-permute-start | bytes 1376264 | tf_op jit(solution)/shard_map/ppermute | solution.py:29
  6.2 9.6 %first_step.1 = (f32[32,16,256]{2,1,0:T(8,128)}, f32[8,8192]{1,0:T(8,128)S(1)}) custom-call(f32[16,8192]{1,0:T(8,128)S(1)} %get-tuple-element.10.x_ref.own_ref, f32[8192,256]{1,0:T(8,128)} %proj_ref.1, s32[1,256]{1,0:T(1,128)S(1)} %get-tuple-element.11.index_ref), custom_call_target="tpu_custom_call" | custom-call | tf_op jit(solution)/shard_map/first_step/pallas_call | solution.py:214
  15.9 4.9 %all-to-all-start = ((f32[32,16,256]{2,1,0:T(8,128)}), f32[32,16,256]{2,1,0:T(8,128)S(1)}, u32[]{:S(2)}, u32[]{:S(2)}) async-start(f32[32,16,256]{2,1,0:T(8,128)} %get-tuple-element.14), calls=%async_computation | async-start | bytes 1048576 | tf_op jit(solution)/shard_map/all_to_all | solution.py:419
  20.8 0.0 copy-done.3
  20.9 0.1 copy.9.near_ref
  20.9 0.0 collective-permute-done.1.other_ref
  20.9 0.0 collective-permute-done.chip_ref
  20.9 0.0 copy-done.2
  20.9 0.0 copy-start
  21.0 0.0 copy-start.1
  21.0 17.8 %near_term.1.near_ref = f32[8,8192]{1,0:T(8,128)S(1)} custom-call(s32[32,8]{1,0:T(8,128)S(1)} %copy.9.near_ref, s32[32]{0:T(128)S(1)} %copy-done.2, f32[8,8192]{1,0:T(8,128)S(1)} %get-tuple-element.12.self_ref, f32[8,14336]{1,0:T(8,128)S(1)} %collective-permute-done.chip_ref, f32[16,8192]{1,0:T(8,128)S(1)} %get-tuple-element.10.x_ref.own_ref, ...), custom_call_target="tpu_custom_call" | custom-call | flops 16777216000 | bytes 2097152 | tf_op jit(solution)/shard_map/near_term/pallas_call | solution.py:343
  38.8 0.0 all-to-all-done.gathered_ref
  38.8 0.0 copy-done
  38.8 0.0 copy-done.1
  38.8 12.5 %far_term.1 = f32[8,8192]{1,0:T(8,128)} custom-call(f32[16,8192]{1,0:T(8,128)S(1)} %get-tuple-element.10.x_ref.own_ref, f32[8,8192]{1,0:T(8,128)S(1)} %near_term.1.near_ref, f32[32,16,256]{2,1,0:T(8,128)S(1)} %all-to-all-done.gathered_ref, s32[30,256]{1,0:T(8,128)S(1)} %copy-done.1, f32[512,256]{1,0:T(8,128)S(1)} %copy-done), custom_call_target="tpu_custom_call" | custom-call | tf_op jit(solution)/shard_map/far_term/pallas_call | solution.py:395
Async XLA Ops:
  0.0 20.8 %copy-start.3 = (s32[32,8]{0,1:T(8,128)S(1)}, s32[32,8]{0,1:T(8,128)}, u32[]{:S(2)}) copy-start(s32[32,8]{0,1:T(8,128)} %param.14) | copy-start | bytes 3076
  0.0 20.9 %copy-start.2 = (s32[32]{0:T(128)S(1)}, s32[32]{0:T(128)}, u32[]{:S(2)}) copy-start(s32[32]{0:T(128)} %count_ref.1) | copy-start | bytes 388
  1.2 19.7 %collective-permute-start.1 = (f32[8,14336]{1,0:T(8,128)S(1)}, f32[8,14336]{1,0:T(8,128)S(1)}, u32[]{:S(2)}, u32[]{:S(2)}) collective-permute-start(f32[8,14336]{1,0:T(8,128)S(1)} %get-tuple-element.13), channel_id=1, source_target_pairs={{1,2},{2,1},{3,4},{4,3},{5,6},{6,5},{7,8},{8,7},{9,10},{10,9},{11,... | collective-permute-start | bytes 1376264 | tf_op jit(solution)/shard_map/ppermute | solution.py:29
  1.9 19.0 %collective-permute-start = (f32[8,14336]{1,0:T(8,128)S(1)}, f32[8,14336]{1,0:T(8,128)S(1)}, u32[]{:S(2)}, u32[]{:S(2)}) collective-permute-start(f32[8,14336]{1,0:T(8,128)S(1)} %get-tuple-element.13), channel_id=1, source_target_pairs={{0,1},{1,0},{2,3},{3,2},{4,5},{5,4},{6,7},{7,6},{8,9},{9,8},{10,11... | collective-permute-start | bytes 1376264 | tf_op jit(solution)/shard_map/ppermute | solution.py:29
  15.9 22.9 %all-to-all-start = ((f32[32,16,256]{2,1,0:T(8,128)}), f32[32,16,256]{2,1,0:T(8,128)S(1)}, u32[]{:S(2)}, u32[]{:S(2)}) async-start(f32[32,16,256]{2,1,0:T(8,128)} %get-tuple-element.14), calls=%async_computation | async-start | bytes 1048576 | tf_op jit(solution)/shard_map/all_to_all | solution.py:419
  20.9 17.8 %copy-start = (f32[512,256]{1,0:T(8,128)S(1)}, f32[512,256]{1,0:T(8,128)}, u32[]{:S(2)}) copy-start(f32[512,256]{1,0:T(8,128)} %transfer_ref.1) | copy-start | bytes 1572868
  21.0 17.8 %copy-start.1 = (s32[30,256]{1,0:T(8,128)S(1)}, s32[30,256]{1,0:T(8,128)}, u32[]{:S(2)}) copy-start(s32[30,256]{1,0:T(8,128)} %selection_ref.1) | copy-start | bytes 92164

commit v5 on v4

--- a/solution.py
+++ b/solution.py
@@ -14,7 +14,7 @@
 SHIFT = 2.0
 NEAR_TURN = 16
 FAR_TURN = 32
-LEAVES_SELF = 32
+LEAVES_SELF = 16
 ROOT = math.sqrt(math.log2(math.e))
 SMEM_SPEC = pl.BlockSpec(memory_space=pltpu.SMEM)
 HBM_SPEC = pl.BlockSpec(memory_space=pltpu.HBM)
@@ -91,10 +91,14 @@
     return total
 
 
-def kernel_pieces(source, target):
+def kernel_pieces(source, target, rows, chunk):
     pieces = []
-    for first in range(0, source.shape[0], LANES):
-        pieces += split_block(jnp.dot(source[first:first + LANES], target, preferred_element_type=F32))
+    for first in range(0, source.shape[0], rows):
+        split = [
+            split_block(jnp.dot(source[at:at + chunk], target, preferred_element_type=F32))
+            for at in range(first, first + rows, chunk)
+        ]
+        pieces += [high for high, _ in split] + [low for _, low in split]
     return pieces
 
 
@@ -275,17 +279,15 @@
 
     front, parts = packed_parts(points)
     last = 3 * (points // 4)
-    for side, ref in enumerate((chip_ref, other_ref)):
-        target = unpacked.at[side]
-        target[0:6, 0:last] = ref[0:6, front]
-        for part, columns in enumerate(parts):
-            target[2 * part:2 * part + 2, last:] = ref[6:8, columns]
-        add_norm(target)
+    unpacked[0:6, 0:last] = other_ref[0:6, front]
+    for part, columns in enumerate(parts):
+        unpacked[2 * part:2 * part + 2, last:] = other_ref[6:8, columns]
+    add_norm(unpacked)
 
     def prepare(at, _):
         columns = pl.ds(pl.multiple_of(at * wide, wide), wide)
         for part, (coords, values) in enumerate(
-            ((unpacked.at[0], chip_ref), (own_ref, own_ref.at[pl.ds(8, 8)]), (unpacked.at[1], other_ref))
+            ((chip_ref, chip_ref.at[pl.ds(8, 8)]), (own_ref, own_ref.at[pl.ds(8, 8)]), (unpacked, other_ref))
         ):
             window = pl.ds(pl.multiple_of(part * points + at * wide, wide), wide)
             sources[:, window] = source_form(coords[0:8, columns])
@@ -312,7 +314,7 @@
             window = pl.ds(pl.multiple_of(place * leaf, leaf), leaf)
             weight = weights[:, pl.ds(pl.multiple_of(place * 2 * leaf, leaf), 2 * leaf)]
             held.append(jnp.where(slot < count_ref[at], weight, jnp.zeros_like(weight)))
-            pieces += kernel_pieces(sources[:, window].T, target)
+            pieces += kernel_pieces(sources[:, window].T, target, LANES, 64)
         out_ref[:, columns] = self_ref[:, columns] + weigh(held, pieces)
 
     def turn(at, _):
@@ -349,7 +351,7 @@
             pltpu.VMEM((48, 3 * points), BF16),
             pltpu.VMEM((16, 6 * points), BF16),
             pltpu.VMEM((48, points), BF16),
-            pltpu.VMEM((2, 8, points), F32),
+            pltpu.VMEM((8, points), F32),
         ],
         cost_estimate=pl.CostEstimate(flops=1000 * entries, bytes_accessed=4 * 64 * points, transcendentals=entries),
         compiler_params=pltpu.CompilerParams(vmem_limit_bytes=32 * 2**20),
@@ -368,7 +370,8 @@
         node = held[first + ((own_index >> level) ^ 1)]
         form = source_form(node[0:8])
         sources[level] = jnp.concatenate([form, jnp.zeros((LANES - 48, rank), BF16)], axis=0).T
-        weights[level] = repeat_blocks(weight_form(node[8:16]))
+        form = weight_form(node[8:16])
+        weights[level] = jnp.concatenate([form, form], axis=1)
         if level < levels - 1:
             rows = devices - (devices >> level)
             climb(held, first, devices >> (level + 1), selection_ref, rows, transfer, nodes, rows)
@@ -381,7 +384,7 @@
             target = jnp.concatenate([target, jnp.zeros((LANES - 48, tile), BF16)], axis=0)
             pieces = []
             for level in range(levels):
-                pieces += kernel_pieces(sources[level], target)
+                pieces += kernel_pieces(sources[level], target, rank, rank)
             total = weigh([weights[level] for level in range(levels)], pieces)
             out_ref[:, columns] = (total + near_ref[:, columns]) * scale
         return 0
@@ -413,7 +416,7 @@
     leaf = coords.shape[1] // leaves
     scale = 1.0 / (slots * leaf) ** 0.5
     extended, packed, skel_index = extend(coords, right_sides, skel_index)
-    chip = swap(packed, "leaf", 0)
+    chip = swap(extended, "leaf", 0)
     other = swap(packed, "leaf", 1)
     node, own_part = first_step(devices, leaf, extended, projection, skel_index)
     gathered = lax.all_to_all(node, "leaf", 0, 0, tiled=True)

time: 51.6 us -> 47.7 us (0.924)
  Pallas kernels: 41.2 us -> 37.3 us
    ppermute x2, starting transfers between devices: 5.03 us -> 1.2 us  [swap(): return lax.ppermute(value, axis, pairs)]
    all_to_all x1, starting transfers between devices: 4.94 us -> 8.72 us  [body(): gathered = lax.all_to_all(node, 'leaf', 0, 0, tiled=True)]
    pallas_call x1, Pallas kernels: 9.64 us -> 6.19 us  [first_step(): pl.pallas_call(functools.partial(first_kernel, leaf), out_shape=(jax.Shap...]
  transfers between devices with their start and end apart: 3 -> 3, of which waited for: 0 -> 0; matrix products, arithmetic and copies ran while one was open for 0% -> 0% of each run, Pallas kernels for 53% -> 51%
where the time goes in v5:
time: 47.7 us; the launch traced here: 47.4 us
  Pallas kernels  37.3 us (78%)
  starting transfers between devices  9.91 us (21%)
    pallas_call x1, Pallas kernels, near_term(): pl.pallas_call(near_kernel, out_shape=jax.ShapeDtypeStruct((8, points), F...  17.9 us
    pallas_call x1, Pallas kernels, far_term(): pl.pallas_call(functools.partial(far_kernel, scale, tile), out_shape=jax....  12.1 us
    all_to_all x1, starting transfers between devices, body(): gathered = lax.all_to_all(node, 'leaf', 0, 0, tiled=True)  8.72 us
    pallas_call x1, Pallas kernels, first_step(): pl.pallas_call(functools.partial(first_kernel, leaf), out_shape=(jax.Shap...  6.19 us
    ppermute x2, starting transfers between devices, swap(): return lax.ppermute(value, axis, pairs)  1.2 us
    pallas_call x1, Pallas kernels, extend(): pl.pallas_call(extend_kernel, out_shape=(pltpu.VMEM((16, points), F32), p...  1.2 us
  transfers between devices with their start and end apart: 3, of which 0 were waited for; matrix products, arithmetic and copies ran while one was open for 0% of the time, Pallas kernels for 51%

profile of v5, /device:TPU:0, one launch (start us, length us, event | category | flops | bytes accessed | tf_op | source)
XLA Modules:
  0.0 47.4 jit_solution(17137188871990472342)
XLA Ops:
  0.0 0.0 copy-start.3
  0.0 0.0 copy-start.2
  0.0 1.2 %extend.1 = (f32[16,8192]{1,0:T(8,128)S(1)}, f32[8,14336]{1,0:T(8,128)S(1)}, s32[1,256]{1,0:T(1,128)S(1)}) custom-call(f32[6,8192]{1,0:T(8,128)} %coords_ref.1, f32[8,8192]{1,0:T(8,128)} %right_ref.1, s32[1,256]{1,0:T(1,128)} %index_hbm.1), custom_call_target="tpu_custom_call" | custom-call | tf_op jit(solution)/shard_map/extend/pallas_call | solution.py:153
  1.2 0.5 %collective-permute-start = (f32[16,8192]{1,0:T(8,128)S(1)}, f32[16,8192]{1,0:T(8,128)S(1)}, u32[]{:S(2)}, u32[]{:S(2)}) collective-permute-start(f32[16,8192]{1,0:T(8,128)S(1)} %get-tuple-element.10.x_ref.own_ref), channel_id=1, source_target_pairs={{0,1},{1,0},{2,3},{3,2},{4,5},{5,4},{6,7},{7,6},{8,9},{9,8},{10,11... | collective-permute-start | bytes 1572872 | tf_op jit(solution)/shard_map/ppermute | solution.py:29
  1.7 0.7 %collective-permute-start.1 = (f32[8,14336]{1,0:T(8,128)S(1)}, f32[8,14336]{1,0:T(8,128)S(1)}, u32[]{:S(2)}, u32[]{:S(2)}) collective-permute-start(f32[8,14336]{1,0:T(8,128)S(1)} %get-tuple-element.13), channel_id=1, source_target_pairs={{1,2},{2,1},{3,4},{4,3},{5,6},{6,5},{7,8},{8,7},{9,10},{10,9},{11,... | collective-permute-start | bytes 1376264 | tf_op jit(solution)/shard_map/ppermute | solution.py:29
  2.4 6.2 %first_step.1 = (f32[32,16,256]{2,1,0:T(8,128)}, f32[8,8192]{1,0:T(8,128)S(1)}) custom-call(f32[16,8192]{1,0:T(8,128)S(1)} %get-tuple-element.10.x_ref.own_ref, f32[8192,256]{1,0:T(8,128)} %proj_ref.1, s32[1,256]{1,0:T(1,128)S(1)} %get-tuple-element.11.index_ref), custom_call_target="tpu_custom_call" | custom-call | tf_op jit(solution)/shard_map/first_step/pallas_call | solution.py:218
  8.6 8.7 %all-to-all-start = ((f32[32,16,256]{2,1,0:T(8,128)}), f32[32,16,256]{2,1,0:T(8,128)S(1)}, u32[]{:S(2)}, u32[]{:S(2)}) async-start(f32[32,16,256]{2,1,0:T(8,128)} %get-tuple-element.14), calls=%async_computation | async-start | bytes 1048576 | tf_op jit(solution)/shard_map/all_to_all | solution.py:422
  17.3 0.0 copy-done.3
  17.4 0.1 copy.9.near_ref
  17.4 0.0 collective-permute-done.1.other_ref
  17.4 0.0 collective-permute-done.chip_ref
  17.4 0.0 copy-done.2
  17.4 0.0 copy-start
  17.5 0.0 copy-start.1
  17.5 17.9 %near_term.1.near_ref = f32[8,8192]{1,0:T(8,128)S(1)} custom-call(s32[32,8]{1,0:T(8,128)S(1)} %copy.9.near_ref, s32[32]{0:T(128)S(1)} %copy-done.2, f32[8,8192]{1,0:T(8,128)S(1)} %get-tuple-element.12.self_ref, f32[16,8192]{1,0:T(8,128)S(1)} %collective-permute-done.chip_ref, f32[16,8192]{1,0:T(8,128)S(1)} %get-tuple-element.10.x_ref.own_ref, ...), custom_call_target="tpu_custom_call" | custom-call | flops 16777216000 | bytes 2097152 | tf_op jit(solution)/shard_map/near_term/pallas_call | solution.py:345
  35.3 0.0 all-to-all-done.gathered_ref
  35.3 0.0 copy-done
  35.4 0.0 copy-done.1
  35.4 12.1 %far_term.1 = f32[8,8192]{1,0:T(8,128)} custom-call(f32[16,8192]{1,0:T(8,128)S(1)} %get-tuple-element.10.x_ref.own_ref, f32[8,8192]{1,0:T(8,128)S(1)} %near_term.1.near_ref, f32[32,16,256]{2,1,0:T(8,128)S(1)} %all-to-all-done.gathered_ref, s32[30,256]{1,0:T(8,128)S(1)} %copy-done.1, f32[512,256]{1,0:T(8,128)S(1)} %copy-done), custom_call_target="tpu_custom_call" | custom-call | tf_op jit(solution)/shard_map/far_term/pallas_call | solution.py:398
Async XLA Ops:
  0.0 17.3 %copy-start.3 = (s32[32,8]{0,1:T(8,128)S(1)}, s32[32,8]{0,1:T(8,128)}, u32[]{:S(2)}) copy-start(s32[32,8]{0,1:T(8,128)} %param.14) | copy-start | bytes 3076
  0.0 17.4 %copy-start.2 = (s32[32]{0:T(128)S(1)}, s32[32]{0:T(128)}, u32[]{:S(2)}) copy-start(s32[32]{0:T(128)} %count_ref.1) | copy-start | bytes 388
  1.2 16.2 %collective-permute-start = (f32[16,8192]{1,0:T(8,128)S(1)}, f32[16,8192]{1,0:T(8,128)S(1)}, u32[]{:S(2)}, u32[]{:S(2)}) collective-permute-start(f32[16,8192]{1,0:T(8,128)S(1)} %get-tuple-element.10.x_ref.own_ref), channel_id=1, source_target_pairs={{0,1},{1,0},{2,3},{3,2},{4,5},{5,4},{6,7},{7,6},{8,9},{9,8},{10,11... | collective-permute-start | bytes 1572872 | tf_op jit(solution)/shard_map/ppermute | solution.py:29
  1.7 15.7 %collective-permute-start.1 = (f32[8,14336]{1,0:T(8,128)S(1)}, f32[8,14336]{1,0:T(8,128)S(1)}, u32[]{:S(2)}, u32[]{:S(2)}) collective-permute-start(f32[8,14336]{1,0:T(8,128)S(1)} %get-tuple-element.13), channel_id=1, source_target_pairs={{1,2},{2,1},{3,4},{4,3},{5,6},{6,5},{7,8},{8,7},{9,10},{10,9},{11,... | collective-permute-start | bytes 1376264 | tf_op jit(solution)/shard_map/ppermute | solution.py:29
  8.6 26.7 %all-to-all-start = ((f32[32,16,256]{2,1,0:T(8,128)}), f32[32,16,256]{2,1,0:T(8,128)S(1)}, u32[]{:S(2)}, u32[]{:S(2)}) async-start(f32[32,16,256]{2,1,0:T(8,128)} %get-tuple-element.14), calls=%async_computation | async-start | bytes 1048576 | tf_op jit(solution)/shard_map/all_to_all | solution.py:422
  17.4 17.9 %copy-start = (f32[512,256]{1,0:T(8,128)S(1)}, f32[512,256]{1,0:T(8,128)}, u32[]{:S(2)}) copy-start(f32[512,256]{1,0:T(8,128)} %transfer_ref.1) | copy-start | bytes 1572868
  17.5 17.9 %copy-start.1 = (s32[30,256]{1,0:T(8,128)S(1)}, s32[30,256]{1,0:T(8,128)}, u32[]{:S(2)}) copy-start(s32[30,256]{1,0:T(8,128)} %selection_ref.1) | copy-start | bytes 92164

commit v6 on v5

--- a/solution.py
+++ b/solution.py
@@ -314,7 +314,7 @@
             window = pl.ds(pl.multiple_of(place * leaf, leaf), leaf)
             weight = weights[:, pl.ds(pl.multiple_of(place * 2 * leaf, leaf), 2 * leaf)]
             held.append(jnp.where(slot < count_ref[at], weight, jnp.zeros_like(weight)))
-            pieces += kernel_pieces(sources[:, window].T, target, LANES, 64)
+            pieces += kernel_pieces(sources[:, window].T, target, LANES, LANES)
         out_ref[:, columns] = self_ref[:, columns] + weigh(held, pieces)
 
     def turn(at, _):
@@ -369,7 +369,8 @@
     for level in range(levels):
         node = held[first + ((own_index >> level) ^ 1)]
         form = source_form(node[0:8])
-        sources[level] = jnp.concatenate([form, jnp.zeros((LANES - 48, rank), BF16)], axis=0).T
+        form = jnp.concatenate([form, jnp.zeros((LANES - 48, rank), BF16)], axis=0)
+        sources[level * rank:(level + 1) * rank] = form.T
         form = weight_form(node[8:16])
         weights[level] = jnp.concatenate([form, form], axis=1)
         if level < levels - 1:
@@ -383,8 +384,11 @@
             target = target_form(own_ref[0:8, columns])
             target = jnp.concatenate([target, jnp.zeros((LANES - 48, tile), BF16)], axis=0)
             pieces = []
-            for level in range(levels):
-                pieces += kernel_pieces(sources[level], target, rank, rank)
+            for level in range(0, levels, 2):
+                pair = sources[level * rank:min(level + 2, levels) * rank]
+                exponent = jnp.dot(pair, target, preferred_element_type=F32)
+                for first in range(0, pair.shape[0], rank):
+                    pieces += split_block(exponent[first:first + rank])
             total = weigh([weights[level] for level in range(levels)], pieces)
             out_ref[:, columns] = (total + near_ref[:, columns]) * scale
         return 0
@@ -402,7 +406,7 @@
         out_specs=VMEM_SPEC,
         scratch_shapes=[
             pltpu.VMEM((devices - 2, 16, rank), F32),
-            pltpu.VMEM((levels, rank, LANES), BF16),
+            pltpu.VMEM((levels * rank, LANES), BF16),
             pltpu.VMEM((levels, 16, 2 * rank), BF16),
         ],
         compiler_params=pltpu.CompilerParams(vmem_limit_bytes=32 * 2**20),

time: 47.7 us -> 47.8 us (level)
  transfers between devices with their start and end apart: 3 -> 3, of which waited for: 0 -> 0; matrix products, arithmetic and copies ran while one was open for 0% -> 0% of each run, Pallas kernels for 51% -> 50%
where the time goes in v6:
time: 47.8 us; the launch traced here: 47.5 us
  Pallas kernels  37.2 us (78%)
  starting transfers between devices  10.1 us (21%)
    pallas_call x1, Pallas kernels, near_term(): pl.pallas_call(near_kernel, out_shape=jax.ShapeDtypeStruct((8, points), F...  17.5 us
    pallas_call x1, Pallas kernels, far_term(): pl.pallas_call(functools.partial(far_kernel, scale, tile), out_shape=jax....  12.3 us
    all_to_all x1, starting transfers between devices, body(): gathered = lax.all_to_all(node, 'leaf', 0, 0, tiled=True)  8.9 us
    pallas_call x1, Pallas kernels, first_step(): pl.pallas_call(functools.partial(first_kernel, leaf), out_shape=(jax.Shap...  6.19 us
    pallas_call x1, Pallas kernels, extend(): pl.pallas_call(extend_kernel, out_shape=(pltpu.VMEM((16, points), F32), p...  1.2 us
    ppermute x2, starting transfers between devices, swap(): return lax.ppermute(value, axis, pairs)  1.2 us
  transfers between devices with their start and end apart: 3, of which 0 were waited for; matrix products, arithmetic and copies ran while one was open for 0% of the time, Pallas kernels for 50%

profile of v6, /device:TPU:0, one launch (start us, length us, event | category | flops | bytes accessed | tf_op | source)
XLA Modules:
  0.0 47.5 jit_solution(8074996092359482779)
XLA Ops:
  0.0 0.0 copy-start.3
  0.0 0.0 copy-start.2
  0.0 1.2 %extend.1 = (f32[16,8192]{1,0:T(8,128)S(1)}, f32[8,14336]{1,0:T(8,128)S(1)}, s32[1,256]{1,0:T(1,128)S(1)}) custom-call(f32[6,8192]{1,0:T(8,128)} %coords_ref.1, f32[8,8192]{1,0:T(8,128)} %right_ref.1, s32[1,256]{1,0:T(1,128)} %index_hbm.1), custom_call_target="tpu_custom_call" | custom-call | tf_op jit(solution)/shard_map/extend/pallas_call | solution.py:153
  1.2 0.5 %collective-permute-start = (f32[16,8192]{1,0:T(8,128)S(1)}, f32[16,8192]{1,0:T(8,128)S(1)}, u32[]{:S(2)}, u32[]{:S(2)}) collective-permute-start(f32[16,8192]{1,0:T(8,128)S(1)} %get-tuple-element.10.x_ref.own_ref), channel_id=1, source_target_pairs={{0,1},{1,0},{2,3},{3,2},{4,5},{5,4},{6,7},{7,6},{8,9},{9,8},{10,11... | collective-permute-start | bytes 1572872 | tf_op jit(solution)/shard_map/ppermute | solution.py:29
  1.7 0.7 %collective-permute-start.1 = (f32[8,14336]{1,0:T(8,128)S(1)}, f32[8,14336]{1,0:T(8,128)S(1)}, u32[]{:S(2)}, u32[]{:S(2)}) collective-permute-start(f32[8,14336]{1,0:T(8,128)S(1)} %get-tuple-element.13), channel_id=1, source_target_pairs={{1,2},{2,1},{3,4},{4,3},{5,6},{6,5},{7,8},{8,7},{9,10},{10,9},{11,... | collective-permute-start | bytes 1376264 | tf_op jit(solution)/shard_map/ppermute | solution.py:29
  2.4 6.2 %first_step.1 = (f32[32,16,256]{2,1,0:T(8,128)}, f32[8,8192]{1,0:T(8,128)S(1)}) custom-call(f32[16,8192]{1,0:T(8,128)S(1)} %get-tuple-element.10.x_ref.own_ref, f32[8192,256]{1,0:T(8,128)} %proj_ref.1, s32[1,256]{1,0:T(1,128)S(1)} %get-tuple-element.11.index_ref), custom_call_target="tpu_custom_call" | custom-call | tf_op jit(solution)/shard_map/first_step/pallas_call | solution.py:218
  8.6 8.9 %all-to-all-start = ((f32[32,16,256]{2,1,0:T(8,128)}), f32[32,16,256]{2,1,0:T(8,128)S(1)}, u32[]{:S(2)}, u32[]{:S(2)}) async-start(f32[32,16,256]{2,1,0:T(8,128)} %get-tuple-element.14), calls=%async_computation | async-start | bytes 1048576 | tf_op jit(solution)/shard_map/all_to_all | solution.py:426
  17.5 0.0 copy-done.3
  17.5 0.1 copy.9.near_ref
  17.6 0.0 collective-permute-done.1.other_ref
  17.6 0.0 collective-permute-done.chip_ref
  17.6 0.0 copy-done.2
  17.6 0.0 copy-start
  17.6 0.0 copy-start.1
  17.6 17.5 %near_term.1.near_ref = f32[8,8192]{1,0:T(8,128)S(1)} custom-call(s32[32,8]{1,0:T(8,128)S(1)} %copy.9.near_ref, s32[32]{0:T(128)S(1)} %copy-done.2, f32[8,8192]{1,0:T(8,128)S(1)} %get-tuple-element.12.self_ref, f32[16,8192]{1,0:T(8,128)S(1)} %collective-permute-done.chip_ref, f32[16,8192]{1,0:T(8,128)S(1)} %get-tuple-element.10.x_ref.own_ref, ...), custom_call_target="tpu_custom_call" | custom-call | flops 16777216000 | bytes 2097152 | tf_op jit(solution)/shard_map/near_term/pallas_call | solution.py:345
  35.2 0.0 all-to-all-done.gathered_ref
  35.2 0.0 copy-done
  35.2 0.0 copy-done.1
  35.2 12.3 %far_term.1 = f32[8,8192]{1,0:T(8,128)} custom-call(f32[16,8192]{1,0:T(8,128)S(1)} %get-tuple-element.10.x_ref.own_ref, f32[8,8192]{1,0:T(8,128)S(1)} %near_term.1.near_ref, f32[32,16,256]{2,1,0:T(8,128)S(1)} %all-to-all-done.gathered_ref, s32[30,256]{1,0:T(8,128)S(1)} %copy-done.1, f32[512,256]{1,0:T(8,128)S(1)} %copy-done), custom_call_target="tpu_custom_call" | custom-call | tf_op jit(solution)/shard_map/far_term/pallas_call | solution.py:402
Async XLA Ops:
  0.0 17.5 %copy-start.3 = (s32[32,8]{0,1:T(8,128)S(1)}, s32[32,8]{0,1:T(8,128)}, u32[]{:S(2)}) copy-start(s32[32,8]{0,1:T(8,128)} %param.14) | copy-start | bytes 3076
  0.0 17.6 %copy-start.2 = (s32[32]{0:T(128)S(1)}, s32[32]{0:T(128)}, u32[]{:S(2)}) copy-start(s32[32]{0:T(128)} %count_ref.1) | copy-start | bytes 388
  1.2 16.4 %collective-permute-start = (f32[16,8192]{1,0:T(8,128)S(1)}, f32[16,8192]{1,0:T(8,128)S(1)}, u32[]{:S(2)}, u32[]{:S(2)}) collective-permute-start(f32[16,8192]{1,0:T(8,128)S(1)} %get-tuple-element.10.x_ref.own_ref), channel_id=1, source_target_pairs={{0,1},{1,0},{2,3},{3,2},{4,5},{5,4},{6,7},{7,6},{8,9},{9,8},{10,11... | collective-permute-start | bytes 1572872 | tf_op jit(solution)/shard_map/ppermute | solution.py:29
  1.7 15.9 %collective-permute-start.1 = (f32[8,14336]{1,0:T(8,128)S(1)}, f32[8,14336]{1,0:T(8,128)S(1)}, u32[]{:S(2)}, u32[]{:S(2)}) collective-permute-start(f32[8,14336]{1,0:T(8,128)S(1)} %get-tuple-element.13), channel_id=1, source_target_pairs={{1,2},{2,1},{3,4},{4,3},{5,6},{6,5},{7,8},{8,7},{9,10},{10,9},{11,... | collective-permute-start | bytes 1376264 | tf_op jit(solution)/shard_map/ppermute | solution.py:29
  8.6 26.6 %all-to-all-start = ((f32[32,16,256]{2,1,0:T(8,128)}), f32[32,16,256]{2,1,0:T(8,128)S(1)}, u32[]{:S(2)}, u32[]{:S(2)}) async-start(f32[32,16,256]{2,1,0:T(8,128)} %get-tuple-element.14), calls=%async_computation | async-start | bytes 1048576 | tf_op jit(solution)/shard_map/all_to_all | solution.py:426
  17.6 17.6 %copy-start = (f32[512,256]{1,0:T(8,128)S(1)}, f32[512,256]{1,0:T(8,128)}, u32[]{:S(2)}) copy-start(f32[512,256]{1,0:T(8,128)} %transfer_ref.1) | copy-start | bytes 1572868
  17.6 17.6 %copy-start.1 = (s32[30,256]{1,0:T(8,128)S(1)}, s32[30,256]{1,0:T(8,128)}, u32[]{:S(2)}) copy-start(s32[30,256]{1,0:T(8,128)} %selection_ref.1) | copy-start | bytes 92164

commit v7 on v5

--- a/solution.py
+++ b/solution.py
@@ -314,7 +314,7 @@
             window = pl.ds(pl.multiple_of(place * leaf, leaf), leaf)
             weight = weights[:, pl.ds(pl.multiple_of(place * 2 * leaf, leaf), 2 * leaf)]
             held.append(jnp.where(slot < count_ref[at], weight, jnp.zeros_like(weight)))
-            pieces += kernel_pieces(sources[:, window].T, target, LANES, 64)
+            pieces += kernel_pieces(sources[:, window].T, target, LANES, LANES)
         out_ref[:, columns] = self_ref[:, columns] + weigh(held, pieces)
 
     def turn(at, _):

time: 47.7 us -> 47.6 us (level)
  transfers between devices with their start and end apart: 3 -> 3, of which waited for: 0 -> 0; matrix products, arithmetic and copies ran while one was open for 0% -> 0% of each run, Pallas kernels for 51% -> 50%
where the time goes in v7:
time: 47.6 us; the launch traced here: 47.3 us
  Pallas kernels  37 us (78%)
  starting transfers between devices  10.1 us (21%)
    pallas_call x1, Pallas kernels, near_term(): pl.pallas_call(near_kernel, out_shape=jax.ShapeDtypeStruct((8, points), F...  17.5 us
    pallas_call x1, Pallas kernels, far_term(): pl.pallas_call(functools.partial(far_kernel, scale, tile), out_shape=jax....  12.1 us
    all_to_all x1, starting transfers between devices, body(): gathered = lax.all_to_all(node, 'leaf', 0, 0, tiled=True)  8.9 us
    pallas_call x1, Pallas kernels, first_step(): pl.pallas_call(functools.partial(first_kernel, leaf), out_shape=(jax.Shap...  6.19 us
    pallas_call x1, Pallas kernels, extend(): pl.pallas_call(extend_kernel, out_shape=(pltpu.VMEM((16, points), F32), p...  1.2 us
    ppermute x2, starting transfers between devices, swap(): return lax.ppermute(value, axis, pairs)  1.2 us
  transfers between devices with their start and end apart: 3, of which 0 were waited for; matrix products, arithmetic and copies ran while one was open for 0% of the time, Pallas kernels for 50%

profile of v7, /device:TPU:0, one launch (start us, length us, event | category | flops | bytes accessed | tf_op | source)
XLA Modules:
  0.0 47.3 jit_solution(17727293905348454560)
XLA Ops:
  0.0 0.0 copy-start.3
  0.0 0.0 copy-start.2
  0.0 1.2 %extend.1 = (f32[16,8192]{1,0:T(8,128)S(1)}, f32[8,14336]{1,0:T(8,128)S(1)}, s32[1,256]{1,0:T(1,128)S(1)}) custom-call(f32[6,8192]{1,0:T(8,128)} %coords_ref.1, f32[8,8192]{1,0:T(8,128)} %right_ref.1, s32[1,256]{1,0:T(1,128)} %index_hbm.1), custom_call_target="tpu_custom_call" | custom-call | tf_op jit(solution)/shard_map/extend/pallas_call | solution.py:153
  1.2 0.5 %collective-permute-start = (f32[16,8192]{1,0:T(8,128)S(1)}, f32[16,8192]{1,0:T(8,128)S(1)}, u32[]{:S(2)}, u32[]{:S(2)}) collective-permute-start(f32[16,8192]{1,0:T(8,128)S(1)} %get-tuple-element.10.x_ref.own_ref), channel_id=1, source_target_pairs={{0,1},{1,0},{2,3},{3,2},{4,5},{5,4},{6,7},{7,6},{8,9},{9,8},{10,11... | collective-permute-start | bytes 1572872 | tf_op jit(solution)/shard_map/ppermute | solution.py:29
  1.7 0.7 %collective-permute-start.1 = (f32[8,14336]{1,0:T(8,128)S(1)}, f32[8,14336]{1,0:T(8,128)S(1)}, u32[]{:S(2)}, u32[]{:S(2)}) collective-permute-start(f32[8,14336]{1,0:T(8,128)S(1)} %get-tuple-element.13), channel_id=1, source_target_pairs={{1,2},{2,1},{3,4},{4,3},{5,6},{6,5},{7,8},{8,7},{9,10},{10,9},{11,... | collective-permute-start | bytes 1376264 | tf_op jit(solution)/shard_map/ppermute | solution.py:29
  2.4 6.2 %first_step.1 = (f32[32,16,256]{2,1,0:T(8,128)}, f32[8,8192]{1,0:T(8,128)S(1)}) custom-call(f32[16,8192]{1,0:T(8,128)S(1)} %get-tuple-element.10.x_ref.own_ref, f32[8192,256]{1,0:T(8,128)} %proj_ref.1, s32[1,256]{1,0:T(1,128)S(1)} %get-tuple-element.11.index_ref), custom_call_target="tpu_custom_call" | custom-call | tf_op jit(solution)/shard_map/first_step/pallas_call | solution.py:218
  8.6 8.9 %all-to-all-start = ((f32[32,16,256]{2,1,0:T(8,128)}), f32[32,16,256]{2,1,0:T(8,128)S(1)}, u32[]{:S(2)}, u32[]{:S(2)}) async-start(f32[32,16,256]{2,1,0:T(8,128)} %get-tuple-element.14), calls=%async_computation | async-start | bytes 1048576 | tf_op jit(solution)/shard_map/all_to_all | solution.py:422
  17.5 0.0 copy-done.3
  17.5 0.1 copy.9.near_ref
  17.6 0.0 collective-permute-done.1.other_ref
  17.6 0.0 collective-permute-done.chip_ref
  17.6 0.0 copy-done.2
  17.6 0.0 copy-start
  17.6 0.0 copy-start.1
  17.6 17.5 %near_term.1.near_ref = f32[8,8192]{1,0:T(8,128)S(1)} custom-call(s32[32,8]{1,0:T(8,128)S(1)} %copy.9.near_ref, s32[32]{0:T(128)S(1)} %copy-done.2, f32[8,8192]{1,0:T(8,128)S(1)} %get-tuple-element.12.self_ref, f32[16,8192]{1,0:T(8,128)S(1)} %collective-permute-done.chip_ref, f32[16,8192]{1,0:T(8,128)S(1)} %get-tuple-element.10.x_ref.own_ref, ...), custom_call_target="tpu_custom_call" | custom-call | flops 16777216000 | bytes 2097152 | tf_op jit(solution)/shard_map/near_term/pallas_call | solution.py:345
  35.2 0.0 all-to-all-done.gathered_ref
  35.2 0.0 copy-done
  35.2 0.0 copy-done.1
  35.2 12.1 %far_term.1 = f32[8,8192]{1,0:T(8,128)} custom-call(f32[16,8192]{1,0:T(8,128)S(1)} %get-tuple-element.10.x_ref.own_ref, f32[8,8192]{1,0:T(8,128)S(1)} %near_term.1.near_ref, f32[32,16,256]{2,1,0:T(8,128)S(1)} %all-to-all-done.gathered_ref, s32[30,256]{1,0:T(8,128)S(1)} %copy-done.1, f32[512,256]{1,0:T(8,128)S(1)} %copy-done), custom_call_target="tpu_custom_call" | custom-call | tf_op jit(solution)/shard_map/far_term/pallas_call | solution.py:398
Async XLA Ops:
  0.0 17.5 %copy-start.3 = (s32[32,8]{0,1:T(8,128)S(1)}, s32[32,8]{0,1:T(8,128)}, u32[]{:S(2)}) copy-start(s32[32,8]{0,1:T(8,128)} %param.14) | copy-start | bytes 3076
  0.0 17.6 %copy-start.2 = (s32[32]{0:T(128)S(1)}, s32[32]{0:T(128)}, u32[]{:S(2)}) copy-start(s32[32]{0:T(128)} %count_ref.1) | copy-start | bytes 388
  1.2 16.4 %collective-permute-start = (f32[16,8192]{1,0:T(8,128)S(1)}, f32[16,8192]{1,0:T(8,128)S(1)}, u32[]{:S(2)}, u32[]{:S(2)}) collective-permute-start(f32[16,8192]{1,0:T(8,128)S(1)} %get-tuple-element.10.x_ref.own_ref), channel_id=1, source_target_pairs={{0,1},{1,0},{2,3},{3,2},{4,5},{5,4},{6,7},{7,6},{8,9},{9,8},{10,11... | collective-permute-start | bytes 1572872 | tf_op jit(solution)/shard_map/ppermute | solution.py:29
  1.7 15.9 %collective-permute-start.1 = (f32[8,14336]{1,0:T(8,128)S(1)}, f32[8,14336]{1,0:T(8,128)S(1)}, u32[]{:S(2)}, u32[]{:S(2)}) collective-permute-start(f32[8,14336]{1,0:T(8,128)S(1)} %get-tuple-element.13), channel_id=1, source_target_pairs={{1,2},{2,1},{3,4},{4,3},{5,6},{6,5},{7,8},{8,7},{9,10},{10,9},{11,... | collective-permute-start | bytes 1376264 | tf_op jit(solution)/shard_map/ppermute | solution.py:29
  8.6 26.6 %all-to-all-start = ((f32[32,16,256]{2,1,0:T(8,128)}), f32[32,16,256]{2,1,0:T(8,128)S(1)}, u32[]{:S(2)}, u32[]{:S(2)}) async-start(f32[32,16,256]{2,1,0:T(8,128)} %get-tuple-element.14), calls=%async_computation | async-start | bytes 1048576 | tf_op jit(solution)/shard_map/all_to_all | solution.py:422
  17.6 17.6 %copy-start = (f32[512,256]{1,0:T(8,128)S(1)}, f32[512,256]{1,0:T(8,128)}, u32[]{:S(2)}) copy-start(f32[512,256]{1,0:T(8,128)} %transfer_ref.1) | copy-start | bytes 1572868
  17.6 17.6 %copy-start.1 = (s32[30,256]{1,0:T(8,128)S(1)}, s32[30,256]{1,0:T(8,128)}, u32[]{:S(2)}) copy-start(s32[30,256]{1,0:T(8,128)} %selection_ref.1) | copy-start | bytes 92164

commit v8 on v7

--- a/solution.py
+++ b/solution.py
@@ -275,7 +275,10 @@
     own_index = lax.axis_index("leaf")
     even = own_index % 2 == 0
     first_leaf = own_index * leaves
-    wide = 8 * leaf
+    wide = 16 * leaf
+    empty = 3 * points
+    sources[:, empty:] = jnp.zeros((48, leaf), BF16)
+    weights[:, 2 * empty:] = jnp.zeros((16, 2 * leaf), BF16)
 
     front, parts = packed_parts(points)
     last = 3 * (points // 4)
@@ -311,9 +314,10 @@
         held, pieces = [], []
         for slot in range(1, live_slots):
             place = window_place(near_ref[at, slot] - first_leaf)
+            place = jnp.where(slot < count_ref[at], place, 3 * leaves)
             window = pl.ds(pl.multiple_of(place * leaf, leaf), leaf)
             weight = weights[:, pl.ds(pl.multiple_of(place * 2 * leaf, leaf), 2 * leaf)]
-            held.append(jnp.where(slot < count_ref[at], weight, jnp.zeros_like(weight)))
+            held.append(weight)
             pieces += kernel_pieces(sources[:, window].T, target, LANES, LANES)
         out_ref[:, columns] = self_ref[:, columns] + weigh(held, pieces)
 
@@ -348,8 +352,8 @@
         in_specs=[SMEM_SPEC] * 2 + [VMEM_SPEC] * 4,
         out_specs=VMEM_SPEC,
         scratch_shapes=[
-            pltpu.VMEM((48, 3 * points), BF16),
-            pltpu.VMEM((16, 6 * points), BF16),
+            pltpu.VMEM((48, 3 * points + points // leaves), BF16),
+            pltpu.VMEM((16, 6 * points + 2 * (points // leaves)), BF16),
             pltpu.VMEM((48, points), BF16),
             pltpu.VMEM((8, points), F32),
         ],

time: 47.6 us -> 47.5 us (level)
  transfers between devices with their start and end apart: 3 -> 3, of which waited for: 0 -> 0; matrix products, arithmetic and copies ran while one was open for 0% -> 0% of each run, Pallas kernels for 50% -> 51%
where the time goes in v8:
time: 47.5 us; the launch traced here: 47.2 us
  Pallas kernels  37.1 us (78%)
  starting transfers between devices  9.91 us (21%)
    pallas_call x1, Pallas kernels, near_term(): pl.pallas_call(near_kernel, out_shape=jax.ShapeDtypeStruct((8, points), F...  17.6 us
    pallas_call x1, Pallas kernels, far_term(): pl.pallas_call(functools.partial(far_kernel, scale, tile), out_shape=jax....  12.1 us
    all_to_all x1, starting transfers between devices, body(): gathered = lax.all_to_all(node, 'leaf', 0, 0, tiled=True)  8.72 us
    pallas_call x1, Pallas kernels, first_step(): pl.pallas_call(functools.partial(first_kernel, leaf), out_shape=(jax.Shap...  6.19 us
    pallas_call x1, Pallas kernels, extend(): pl.pallas_call(extend_kernel, out_shape=(pltpu.VMEM((16, points), F32), p...  1.2 us
    ppermute x2, starting transfers between devices, swap(): return lax.ppermute(value, axis, pairs)  1.2 us
  transfers between devices with their start and end apart: 3, of which 0 were waited for; matrix products, arithmetic and copies ran while one was open for 0% of the time, Pallas kernels for 51%

profile of v8, /device:TPU:0, one launch (start us, length us, event | category | flops | bytes accessed | tf_op | source)
XLA Modules:
  0.0 47.2 jit_solution(5332028436666484118)
XLA Ops:
  0.0 0.0 copy-start.3
  0.0 0.0 copy-start.2
  0.0 1.2 %extend.1 = (f32[16,8192]{1,0:T(8,128)S(1)}, f32[8,14336]{1,0:T(8,128)S(1)}, s32[1,256]{1,0:T(1,128)S(1)}) custom-call(f32[6,8192]{1,0:T(8,128)} %coords_ref.1, f32[8,8192]{1,0:T(8,128)} %right_ref.1, s32[1,256]{1,0:T(1,128)} %index_hbm.1), custom_call_target="tpu_custom_call" | custom-call | tf_op jit(solution)/shard_map/extend/pallas_call | solution.py:153
  1.2 0.5 %collective-permute-start = (f32[16,8192]{1,0:T(8,128)S(1)}, f32[16,8192]{1,0:T(8,128)S(1)}, u32[]{:S(2)}, u32[]{:S(2)}) collective-permute-start(f32[16,8192]{1,0:T(8,128)S(1)} %get-tuple-element.10.x_ref.own_ref), channel_id=1, source_target_pairs={{0,1},{1,0},{2,3},{3,2},{4,5},{5,4},{6,7},{7,6},{8,9},{9,8},{10,11... | collective-permute-start | bytes 1572872 | tf_op jit(solution)/shard_map/ppermute | solution.py:29
  1.7 0.7 %collective-permute-start.1 = (f32[8,14336]{1,0:T(8,128)S(1)}, f32[8,14336]{1,0:T(8,128)S(1)}, u32[]{:S(2)}, u32[]{:S(2)}) collective-permute-start(f32[8,14336]{1,0:T(8,128)S(1)} %get-tuple-element.13), channel_id=1, source_target_pairs={{1,2},{2,1},{3,4},{4,3},{5,6},{6,5},{7,8},{8,7},{9,10},{10,9},{11,... | collective-permute-start | bytes 1376264 | tf_op jit(solution)/shard_map/ppermute | solution.py:29
  2.4 6.2 %first_step.1 = (f32[32,16,256]{2,1,0:T(8,128)}, f32[8,8192]{1,0:T(8,128)S(1)}) custom-call(f32[16,8192]{1,0:T(8,128)S(1)} %get-tuple-element.10.x_ref.own_ref, f32[8192,256]{1,0:T(8,128)} %proj_ref.1, s32[1,256]{1,0:T(1,128)S(1)} %get-tuple-element.11.index_ref), custom_call_target="tpu_custom_call" | custom-call | tf_op jit(solution)/shard_map/first_step/pallas_call | solution.py:218
  8.6 8.7 %all-to-all-start = ((f32[32,16,256]{2,1,0:T(8,128)}), f32[32,16,256]{2,1,0:T(8,128)S(1)}, u32[]{:S(2)}, u32[]{:S(2)}) async-start(f32[32,16,256]{2,1,0:T(8,128)} %get-tuple-element.14), calls=%async_computation | async-start | bytes 1048576 | tf_op jit(solution)/shard_map/all_to_all | solution.py:426
  17.3 0.0 copy-done.3
  17.4 0.1 copy.9.near_ref
  17.4 0.0 collective-permute-done.1.other_ref
  17.4 0.0 collective-permute-done.chip_ref
  17.4 0.0 copy-done.2
  17.4 0.0 copy-start
  17.5 0.0 copy-start.1
  17.5 17.6 %near_term.1.near_ref = f32[8,8192]{1,0:T(8,128)S(1)} custom-call(s32[32,8]{1,0:T(8,128)S(1)} %copy.9.near_ref, s32[32]{0:T(128)S(1)} %copy-done.2, f32[8,8192]{1,0:T(8,128)S(1)} %get-tuple-element.12.self_ref, f32[16,8192]{1,0:T(8,128)S(1)} %collective-permute-done.chip_ref, f32[16,8192]{1,0:T(8,128)S(1)} %get-tuple-element.10.x_ref.own_ref, ...), custom_call_target="tpu_custom_call" | custom-call | flops 16777216000 | bytes 2097152 | tf_op jit(solution)/shard_map/near_term/pallas_call | solution.py:349
  35.1 0.0 all-to-all-done.gathered_ref
  35.1 0.0 copy-done
  35.1 0.0 copy-done.1
  35.1 12.1 %far_term.1 = f32[8,8192]{1,0:T(8,128)} custom-call(f32[16,8192]{1,0:T(8,128)S(1)} %get-tuple-element.10.x_ref.own_ref, f32[8,8192]{1,0:T(8,128)S(1)} %near_term.1.near_ref, f32[32,16,256]{2,1,0:T(8,128)S(1)} %all-to-all-done.gathered_ref, s32[30,256]{1,0:T(8,128)S(1)} %copy-done.1, f32[512,256]{1,0:T(8,128)S(1)} %copy-done), custom_call_target="tpu_custom_call" | custom-call | tf_op jit(solution)/shard_map/far_term/pallas_call | solution.py:402
Async XLA Ops:
  0.0 17.3 %copy-start.3 = (s32[32,8]{0,1:T(8,128)S(1)}, s32[32,8]{0,1:T(8,128)}, u32[]{:S(2)}) copy-start(s32[32,8]{0,1:T(8,128)} %param.14) | copy-start | bytes 3076
  0.0 17.4 %copy-start.2 = (s32[32]{0:T(128)S(1)}, s32[32]{0:T(128)}, u32[]{:S(2)}) copy-start(s32[32]{0:T(128)} %count_ref.1) | copy-start | bytes 388
  1.2 16.2 %collective-permute-start = (f32[16,8192]{1,0:T(8,128)S(1)}, f32[16,8192]{1,0:T(8,128)S(1)}, u32[]{:S(2)}, u32[]{:S(2)}) collective-permute-start(f32[16,8192]{1,0:T(8,128)S(1)} %get-tuple-element.10.x_ref.own_ref), channel_id=1, source_target_pairs={{0,1},{1,0},{2,3},{3,2},{4,5},{5,4},{6,7},{7,6},{8,9},{9,8},{10,11... | collective-permute-start | bytes 1572872 | tf_op jit(solution)/shard_map/ppermute | solution.py:29
  1.7 15.7 %collective-permute-start.1 = (f32[8,14336]{1,0:T(8,128)S(1)}, f32[8,14336]{1,0:T(8,128)S(1)}, u32[]{:S(2)}, u32[]{:S(2)}) collective-permute-start(f32[8,14336]{1,0:T(8,128)S(1)} %get-tuple-element.13), channel_id=1, source_target_pairs={{1,2},{2,1},{3,4},{4,3},{5,6},{6,5},{7,8},{8,7},{9,10},{10,9},{11,... | collective-permute-start | bytes 1376264 | tf_op jit(solution)/shard_map/ppermute | solution.py:29
  8.6 26.5 %all-to-all-start = ((f32[32,16,256]{2,1,0:T(8,128)}), f32[32,16,256]{2,1,0:T(8,128)S(1)}, u32[]{:S(2)}, u32[]{:S(2)}) async-start(f32[32,16,256]{2,1,0:T(8,128)} %get-tuple-element.14), calls=%async_computation | async-start | bytes 1048576 | tf_op jit(solution)/shard_map/all_to_all | solution.py:426
  17.4 17.7 %copy-start = (f32[512,256]{1,0:T(8,128)S(1)}, f32[512,256]{1,0:T(8,128)}, u32[]{:S(2)}) copy-start(f32[512,256]{1,0:T(8,128)} %transfer_ref.1) | copy-start | bytes 1572868
  17.5 17.7 %copy-start.1 = (s32[30,256]{1,0:T(8,128)S(1)}, s32[30,256]{1,0:T(8,128)}, u32[]{:S(2)}) copy-start(s32[30,256]{1,0:T(8,128)} %selection_ref.1) | copy-start | bytes 92164
